TPU v7x, 128 devices: a whole 4x4x4 slice. The times are simulated.
128 devices in a mesh: sx: 8 (over y, z_hi), sy: 16 (over z_lo, x, core).
Axes of the slice: x: 4, y: 4, z: 4 (z_hi: 2, z_lo: 2; z = z_hi * 2 + z_lo), core: 2. Of those that a mesh axis runs over, the one named last changes fastest.
Arguments:
- quad_features: bfloat16 [8, 16, 16384, 64], P('sx', 'sy'), may hold values from -6 to 6
- w_first: bfloat16 [64, 512], replicated, may hold values from -0.75 to 0.75
- w_second: bfloat16 [512, 512], replicated, may hold values from -0.25 to 0.25
- w_third: bfloat16 [512, 128], replicated, may hold values from -0.25 to 0.25
- quad_block: int32 [8, 16, 16384], P('sx', 'sy'), may hold values from 0 to 255
- diag_tiles: float32 [64, 64, 16, 2048], P(None, None, 'sx', 'sy'), may hold values from -0.0078125 to 0.0078125
- x_tiles: float32 [64, 64, 16, 2048], P(None, None, 'sx', 'sy'), may hold values from -0.48125 to 0.03125
- y_tiles: float32 [64, 64, 16, 2048], P(None, None, 'sx', 'sy'), may hold values from -0.48125 to 0.03125
- p_tiles: float32 [64, 64, 16, 2048], P(None, None, 'sx', 'sy'), may hold values from -0.48125 to 0.03125
- tile_cols: int32 [8, 16, 256], P('sx', 'sy'), may hold values from 0 to 255, each once within a row
- x_map: int32 [8, 16, 128], P('sx', 'sy'), may hold values from 0 to 127, each once within a row
- y_map: int32 [8, 16, 2], P('sx', 'sy'), may hold values from 0 to 1, each once within a row
Outputs:
- adjoint: float32 [64, 16, 2048], P(None, 'sx', 'sy')
- residual: float32 [64, 16, 2048], P(None, 'sx', 'sy')
Inputs may be any that keep to these rules, and one draw needn't show every extreme that they name: `quad_block`: each entry names a local block of the receiving subdomain. `tile_cols`: each subdomain's row is a permutation of its 256 local blocks. `x_map`: each subdomain's row is a permutation of 0 to 127. `y_map`: each subdomain's row is a permutation of 0 to 1.
All inputs are finite; a program needn't handle non-finite values.
Results may differ from a plain program's by a relative error of at most 0.0038.
Values may be sent and summed in bfloat16 or wider, within the bound.
A program may use at most 192 MiB of HBM per device.

v0:
```python
import jax
import jax.numpy as jnp
from jax import lax
from jax.sharding import PartitionSpec as P

BLOCK_DOFS = 64
FEATURES = 64
ITERS = 3
PER_BLOCK = 64


HIGHEST = lax.Precision.HIGHEST
DIAG_SHIFT = 5.0


def with_halo(block, sides, width):
    for axis, dim in sides:
        count = lax.axis_size(axis)
        forward = [(i, i + 1) for i in range(count - 1)]
        backward = [(target, source) for source, target in forward]
        low = lax.ppermute(
            lax.slice_in_dim(block, block.shape[dim] - width, None, axis=dim), axis, forward
        )
        high = lax.ppermute(lax.slice_in_dim(block, 0, width, axis=dim), axis, backward)
        block = jnp.concatenate([low, block, high], axis=dim)
    return block


def apply_tiles(tile_set, vector):
    return jnp.einsum("ijab,jab->iab", tile_set, vector, precision=HIGHEST)


def apply_transposed(tile_set, vector):
    return jnp.einsum("jiab,jab->iab", tile_set, vector, precision=HIGHEST)


def constitutive(features, w_first, w_second, w_third):
    hidden_one = jax.nn.silu(jnp.dot(features, w_first, preferred_element_type=jnp.float32)).astype(
        jnp.bfloat16
    )
    hidden_two = jax.nn.silu(
        jnp.dot(hidden_one, w_second, preferred_element_type=jnp.float32)
    ).astype(jnp.bfloat16)
    output = jnp.dot(hidden_two, w_third, preferred_element_type=jnp.float32)
    stress = output[:, :BLOCK_DOFS]
    tangent = jax.nn.softplus(output[:, BLOCK_DOFS:]) / PER_BLOCK
    return jnp.concatenate([stress, tangent], axis=1).astype(jnp.bfloat16)


def residual_norm(residual, precond):
    return lax.psum(jnp.sum(residual * precond), ("sx", "sy"))


def local(
    quad_features,
    w_first,
    w_second,
    w_third,
    quad_block,
    diag_tiles,
    x_tiles,
    y_tiles,
    p_tiles,
    tile_cols,
    x_map,
    y_map,
):
    sample_count = quad_features.shape[2]
    devices = lax.axis_size(("sx", "sy"))
    slot_count = sample_count // devices
    row_width = 2 * BLOCK_DOFS
    features = quad_features.reshape(sample_count, FEATURES)
    produced = constitutive(features, w_first, w_second, w_third).reshape(
        devices, slot_count, row_width
    )
    received = lax.all_to_all(produced, ("sx", "sy"), split_axis=0, concat_axis=0, tiled=True)
    received = received.reshape(sample_count, row_width)
    blocks_x = diag_tiles.shape[2]
    blocks_y = diag_tiles.shape[3]
    blocks = blocks_x * blocks_y
    owner_block = quad_block[0, 0]
    onehot = (owner_block[None, :] == jnp.arange(blocks, dtype=jnp.int32)[:, None]).astype(
        jnp.bfloat16
    )
    fields = jnp.dot(onehot, received, preferred_element_type=jnp.float32).T.reshape(
        row_width, blocks_x, blocks_y
    )
    load_vector = fields[:BLOCK_DOFS]
    tangent_sum = fields[BLOCK_DOFS:]
    diagonal = DIAG_SHIFT + tangent_sum
    sym_tiles = diag_tiles + diag_tiles.transpose(1, 0, 2, 3)
    jacobi = diagonal + 2.0 * jnp.moveaxis(jnp.diagonal(diag_tiles, axis1=0, axis2=1), -1, 0)
    columns = tile_cols[0, 0]
    inverse_cols = jnp.argsort(columns)
    map_first = x_map[0, 0]
    inverse_first = jnp.argsort(map_first)
    map_second = y_map[0, 0]
    inverse_second = jnp.argsort(map_second)
    adjoint = jnp.zeros_like(load_vector)
    residual = load_vector
    precond = residual / jacobi
    direction = precond
    rho_now = residual_norm(residual, precond)
    for sweep in range(ITERS):
        result = diagonal * direction + apply_tiles(sym_tiles, direction)
        transposed_x = apply_transposed(x_tiles, direction)
        outgoing_x = jnp.take(transposed_x[:, -1, :], inverse_first, axis=1)
        rim_first = jnp.stack([direction[:, 0, :], outgoing_x], axis=1)
        padded_x = with_halo(rim_first, (("sx", 1),), 1)
        beyond_x = jnp.take(padded_x[:, 3, :], map_first, axis=1)
        partner_x = jnp.concatenate([direction[:, 1:, :], beyond_x[:, None, :]], axis=1)
        result = result + apply_tiles(x_tiles, partner_x)
        result = result + jnp.concatenate([padded_x[:, 0:1, :], transposed_x[:, :-1, :]], axis=1)
        transposed_y = apply_transposed(y_tiles, direction)
        outgoing_y = jnp.take(transposed_y[:, :, -1], inverse_second, axis=1)
        rim_second = jnp.stack([direction[:, :, 0], outgoing_y], axis=2)
        padded_y = with_halo(rim_second, (("sy", 2),), 1)
        beyond_y = jnp.take(padded_y[:, :, 3], map_second, axis=1)
        partner_y = jnp.concatenate([direction[:, :, 1:], beyond_y[:, :, None]], axis=2)
        result = result + apply_tiles(y_tiles, partner_y)
        result = result + jnp.concatenate([padded_y[:, :, 0:1], transposed_y[:, :, :-1]], axis=2)
        flat_vector = direction.reshape(BLOCK_DOFS, blocks)
        gathered = jnp.take(flat_vector, columns, axis=1).reshape(direction.shape)
        result = result + apply_tiles(p_tiles, gathered)
        transposed_p = apply_transposed(p_tiles, direction).reshape(BLOCK_DOFS, blocks)
        result = result + jnp.take(transposed_p, inverse_cols, axis=1).reshape(direction.shape)
        step_size = rho_now / lax.psum(jnp.sum(direction * result), ("sx", "sy"))
        adjoint = adjoint + step_size * direction
        residual = residual - step_size * result
        if sweep + 1 < ITERS:
            precond = residual / jacobi
            rho_next = residual_norm(residual, precond)
            direction = precond + rho_next / rho_now * direction
            rho_now = rho_next
    return (adjoint, residual)


def solution(mesh):
    in_specs = (
        P("sx", "sy", None, None),
        P(),
        P(),
        P(),
        P("sx", "sy", None),
        P(None, None, "sx", "sy"),
        P(None, None, "sx", "sy"),
        P(None, None, "sx", "sy"),
        P(None, None, "sx", "sy"),
        P("sx", "sy", None),
        P("sx", "sy", None),
        P("sx", "sy", None),
    )
    out_specs = (P(None, "sx", "sy"), P(None, "sx", "sy"))
    return jax.shard_map(local, mesh=mesh, in_specs=in_specs, out_specs=out_specs, check_vma=False)
```

profile of v0, /device:TPU:1, one launch (start us, length us, event | category | flops | bytes accessed | tf_op | source)
XLA Modules:
  0.0 594.7 jit_solution(11811576863092225127)
XLA Ops:
  0.7 1.6 copy-done
  2.2 22.2 %fusion = f32[16384,512]{1,0:T(8,128)} fusion(bf16[512,512]{1,0:T(8,128)(2,1)} %param.20, bf16[64,512]{1,0:T(8,128)(2,1)} %param.19, bf16[1,1,16384,64]{2,3,1,0:T(8,128)(2,1)S(1)} %copy-done), kind=kOutput, calls=%fused_computation.22 | convolution fusion | flops 9705619456 | bytes 36241408 | tf_op jit(solution)/shard_map/dot_general | solution.py:42
  24.4 17.9 %fusion.2 = f32[16384,128]{0,1:T(8,128)} fusion(bf16[512,128]{1,0:T(8,128)(2,1)S(1)} %copy-done.6, f32[16384,512]{1,0:T(8,128)} %fusion), kind=kOutput, calls=%fused_computation.24 | convolution fusion | flops 2189426688 | bytes 42074112 | tf_op jit(solution)/shard_map/dot_general | solution.py:44
  42.3 4.8 copy_bitcast_fusion
  47.1 2.4 pad_maximum_fusion
  49.5 12.4 %all-to-all-start = ((bf16[128,128,128]{1,2,0:T(8,128)(2,1)}), bf16[128,128,128]{1,2,0:T(8,128)(2,1)}, u32[]{:S(2)}, u32[]{:S(2)}) async-start(bf16[128,128,128]{1,2,0:T(8,128)(2,1)} %pad_maximum_fusion), calls=%async_computation | async-start | bytes 8388608 | tf_op jit(solution)/shard_map/all_to_all | solution.py:76
  61.9 2.9 gather_fusion
  64.9 3.2 sort.53
  68.1 2.5 sort.51
  71.4 42.9 %all-to-all-done = bf16[128,128,128]{1,2,0:T(8,128)(2,1)} async-done(((bf16[128,128,128]{1,2,0:T(8,128)(2,1)}), bf16[128,128,128]{1,2,0:T(8,128)(2,1)}, u32[]{:S(2)}, u32[]{:S(2)}) %all-to-all-start) | async-done | bytes 4194336 | tf_op jit(solution)/shard_map/all_to_all | solution.py:76
  114.3 6.4 %copy.96 = bf16[128,128,128]{2,1,0:T(8,128)(2,1)} copy(bf16[128,128,128]{1,2,0:T(8,128)(2,1)} %all-to-all-done) | data formatting | bytes 8388608 | tf_op jit(solution)/shard_map/all_to_all | solution.py:76
  120.7 5.5 fusion.1
  126.6 1.6 collective-permute-start
  128.2 2.9 collective-permute-start.2
  131.1 6.0 %multiply_reduce_fusion.20 = f32[2,128,64]{1,0,2:T(2,128)S(1)} fusion(f32[2,128,64]{1,0,2:T(2,128)S(1)} %bitcast.290, f32[64,64,2,128]{3,2,1,0:T(2,128)} %param.23), kind=kLoop, calls=%fused_computation.54 | loop fusion | flops 3129344 | bytes 4325376 | tf_op jit(solution)/shard_map/ijab,jab->iab/dot_general | solution.py:30
  137.0 7.7 %multiply_reduce_fusion.16 = (f32[2,128,64]{1,0,2:T(2,128)S(1)}, f32[2,128,64]{1,0,2:T(2,128)S(1)}, f32[2,128,64]{1,0,2:T(2,128)S(1)}) fusion(f32[64,64,2,128]{3,2,1,0:T(2,128)} %param.25, f32[2,128,64]{1,0,2:T(2,128)S(1)} %bitcast.291, f32[64,64,2,128]{3,2,1,0:T(2,128)S(1)} %copy-done.2, f32[64,64,2,128]{3,2,1,0:T(2,128)} %param.24), kind=kLoop, calls=%fused_computation.50 | loop fusion | flops 6242304 | bytes 12845056 | tf_op jit(solution)/shard_map/jiab,jab->iab/dot_general | solution.py:34
  144.9 0.7 gather_fusion.6
  146.7 5.8 collective-permute-start.1
  153.5 3.1 collective-permute-start.3
  157.5 4.5 multiply_reduce_fusion.15
  163.1 4.5 multiply_reduce_fusion.17
  168.5 4.5 multiply_reduce_fusion.19
  173.0 0.8 multiply_reduce_fusion.25
  173.9 64.2 %all-reduce = (f32[]{:T(128)}, f32[]{:T(128)}) all-reduce(f32[]{:T(128)} %get-tuple-element.20, f32[]{:T(128)} %get-tuple-element.19), channel_id=1, replica_groups=mesh['sx'=8,'sy'=16] {'sx','sy'}, use_global_device_ids=true, to_apply=%region_1.2 | all-reduce | flops 2 | bytes 16 | tf_op jit(solution)/shard_map/psum | solution.py:51
  240.1 62.7 %psum.44 = f32[]{:T(128)} all-reduce(f32[]{:T(128)} %get-tuple-element.33), channel_id=1, replica_groups=mesh['sx'=8,'sy'=16] {'sx','sy'}, use_global_device_ids=true, to_apply=%region_8.12 | all-reduce | flops 1 | bytes 8 | tf_op jit(solution)/shard_map/psum | solution.py:51
  304.5 8.6 %multiply_reduce_fusion.9 = (f32[2,128,64]{1,0,2:T(2,128)S(1)}, f32[2,128,64]{1,0,2:T(2,128)S(1)}, f32[2,128,64]{1,0,2:T(2,128)S(1)}) fusion(f32[64,64,2,128]{3,2,1,0:T(2,128)} %param.25, f32[2,128,64]{1,0,2:T(2,128)S(1)} %bitcast.285, f32[64,64,2,128]{3,2,1,0:T(2,128)} %param.26, f32[64,64,2,128]{3,2,1,0:T(2,128)} %param.24), kind=kLoop, calls=%fused_computation.43 | loop fusion | flops 6242304 | bytes 12845056 | tf_op jit(solution)/shard_map/jiab,jab->iab/dot_general | solution.py:34
  313.1 2.6 multiply_reduce_fusion.13
  315.7 1.3 collective-permute-start.4
  317.0 2.5 collective-permute-start.6
  321.5 4.5 multiply_reduce_fusion.8
  326.9 5.8 collective-permute-start.5
  333.6 3.4 collective-permute-start.7
  338.1 4.5 multiply_reduce_fusion.10
  343.5 4.5 multiply_reduce_fusion.12
  348.0 0.8 multiply_reduce_fusion.23
  348.8 65.9 %psum.45 = f32[]{:T(128)} all-reduce(f32[]{:T(128)} %get-tuple-element.31), channel_id=1, replica_groups=mesh['sx'=8,'sy'=16] {'sx','sy'}, use_global_device_ids=true, to_apply=%region_10.14 | all-reduce | flops 1 | bytes 8 | tf_op jit(solution)/shard_map/psum | solution.py:127
  416.7 62.8 %psum.46 = f32[]{:T(128)} all-reduce(f32[]{:T(128)} %get-tuple-element.28), channel_id=1, replica_groups=mesh['sx'=8,'sy'=16] {'sx','sy'}, use_global_device_ids=true, to_apply=%region_12.16 | all-reduce | flops 1 | bytes 8 | tf_op jit(solution)/shard_map/psum | solution.py:51
  481.2 8.6 %multiply_reduce_fusion.2 = (f32[2,128,64]{1,0,2:T(2,128)S(1)}, f32[2,128,64]{1,0,2:T(2,128)S(1)}, f32[2,128,64]{1,0,2:T(2,128)S(1)}) fusion(f32[64,64,2,128]{3,2,1,0:T(2,128)} %param.25, f32[2,128,64]{1,0,2:T(2,128)S(1)} %bitcast.297, f32[64,64,2,128]{3,2,1,0:T(2,128)} %param.26, f32[64,64,2,128]{3,2,1,0:T(2,128)} %param.24), kind=kLoop, calls=%fused_computation.36 | loop fusion | flops 6242304 | bytes 12845056 | tf_op jit(solution)/shard_map/jiab,jab->iab/dot_general | solution.py:34
  489.8 2.6 multiply_reduce_fusion.6
  492.4 1.3 collective-permute-start.8
  493.7 2.5 collective-permute-start.10
  498.2 4.5 multiply_reduce_fusion.1
  503.6 5.8 collective-permute-start.9
  510.3 3.5 collective-permute-start.11
  514.9 4.6 multiply_reduce_fusion.3
  520.4 4.5 multiply_reduce_fusion.5
  524.9 0.8 multiply_reduce_fusion.21
  525.7 65.9 %psum.47 = f32[]{:T(128)} all-reduce(f32[]{:T(128)} %get-tuple-element.26), channel_id=1, replica_groups=mesh['sx'=8,'sy'=16] {'sx','sy'}, use_global_device_ids=true, to_apply=%region_14.18 | all-reduce | flops 1 | bytes 8 | tf_op jit(solution)/shard_map/psum | solution.py:127
  (153 shorter events, 20.7 us)
Async XLA Ops:
  0.6 1.6 copy-start
  0.6 23.8 %copy-start.6 = (bf16[512,128]{1,0:T(8,128)(2,1)S(1)}, bf16[512,128]{1,0:T(8,128)(2,1)}, u32[]{:S(2)}) copy-start(bf16[512,128]{1,0:T(8,128)(2,1)} %param.21) | copy-start | bytes 393220
  49.5 15.3 %copy-start.5 = (s32[1,1,256]{2,1,0:T(1,128)S(1)}, s32[1,1,256]{2,1,0:T(1,128)}, u32[]{:S(2)}) copy-start(s32[1,1,256]{2,1,0:T(1,128)} %param.27) | copy-start | bytes 3076
  49.5 18.5 %copy-start.8 = (s32[1,1,128]{2,1,0:T(1,128)S(1)}, s32[1,1,128]{2,1,0:T(1,128)}, u32[]{:S(2)}) copy-start(s32[1,1,128]{2,1,0:T(1,128)} %param.28) | copy-start | bytes 1540
  49.5 21.1 %copy-start.9 = (s32[1,1,2]{2,1,0:T(1,128)S(1)}, s32[1,1,2]{2,1,0:T(1,128)}, u32[]{:S(2)}) copy-start(s32[1,1,2]{2,1,0:T(1,128)} %param.29) | copy-start | bytes 28
  49.5 64.8 %all-to-all-start = ((bf16[128,128,128]{1,2,0:T(8,128)(2,1)}), bf16[128,128,128]{1,2,0:T(8,128)(2,1)}, u32[]{:S(2)}, u32[]{:S(2)}) async-start(bf16[128,128,128]{1,2,0:T(8,128)(2,1)} %pad_maximum_fusion), calls=%async_computation | async-start | bytes 8388608 | tf_op jit(solution)/shard_map/all_to_all | solution.py:76
  71.4 49.3 %copy-start.7 = (s32[1,1,16384]{2,1,0:T(1,128)S(1)}, s32[1,1,16384]{2,1,0:T(1,128)}, u32[]{:S(2)}) copy-start(s32[1,1,16384]{2,1,0:T(1,128)} %param.22) | copy-start | bytes 196612
  126.6 10.4 %copy-start.2 = (f32[64,64,2,128]{3,2,1,0:T(2,128)S(1)}, f32[64,64,2,128]{3,2,1,0:T(2,128)}, u32[]{:S(2)}) copy-start(f32[64,64,2,128]{3,2,1,0:T(2,128)} %param.26) | copy-start | bytes 12582916
  126.6 41.0 %collective-permute-start = (f32[64,1,128]{2,1,0:T(1,128)S(1)}, f32[64,1,128]{2,1,0:T(1,128)S(1)}, u32[]{:S(2)}, u32[]{:S(2)}) collective-permute-start(f32[64,1,128]{2,1,0:T(1,128)S(1)} %get-tuple-element.48), channel_id=1, source_target_pairs={{16,0},{32,16},{48,32},{64,48},{80,64},{96,80},{112,96},{17,1},{33... | collective-permute-start | bytes 98312 | tf_op jit(solution)/shard_map/ppermute | solution.py:24
  128.2 33.9 %collective-permute-start.2 = (f32[64,2,1]{2,1,0:T(2,128)S(1)}, f32[64,2,1]{2,1,0:T(2,128)S(1)}, u32[]{:S(2)}, u32[]{:S(2)}) collective-permute-start(f32[64,2,1]{2,1,0:T(2,128)S(1)} %bitcast.289), channel_id=1, source_target_pairs={{1,0},{2,1},{3,2},{4,3},{5,4},{6,5},{7,6},{8,7},{9,8},{10,9},{11,1... | collective-permute-start | bytes 1544 | tf_op jit(solution)/shard_map/ppermute | solution.py:24
  146.7 26.3 %collective-permute-start.1 = (f32[64,1,128]{2,1,0:T(1,128)S(1)}, f32[64,1,128]{2,1,0:T(1,128)S(1)}, u32[]{:S(2)}, u32[]{:S(2)}) collective-permute-start(f32[64,1,128]{2,1,0:T(1,128)S(1)} %bitcast.338), channel_id=1, source_target_pairs={{0,16},{16,32},{32,48},{48,64},{64,80},{80,96},{96,112},{1,17},{17... | collective-permute-start | bytes 98312 | tf_op jit(solution)/shard_map/ppermute | solution.py:21
  153.5 19.5 %collective-permute-start.3 = (f32[64,2,1]{2,1,0:T(2,128)S(1)}, f32[64,2,1]{2,1,0:T(2,128)S(1)}, u32[]{:S(2)}, u32[]{:S(2)}) collective-permute-start(f32[64,2,1]{2,1,0:T(2,128)S(1)} %copy.105), channel_id=1, source_target_pairs={{0,1},{1,2},{2,3},{3,4},{4,5},{5,6},{6,7},{7,8},{8,9},{9,10},{10,1... | collective-permute-start | bytes 1544 | tf_op jit(solution)/shard_map/ppermute | solution.py:21
  304.5 8.6 %copy-start.3 = (f32[64,64,2,128]{3,2,1,0:T(2,128)S(1)}, f32[64,64,2,128]{3,2,1,0:T(2,128)}, u32[]{:S(2)}) copy-start(f32[64,64,2,128]{3,2,1,0:T(2,128)} %param.23) | copy-start | bytes 12582916
  315.7 26.8 %collective-permute-start.4 = (f32[64,1,128]{2,1,0:T(1,128)S(1)}, f32[64,1,128]{2,1,0:T(1,128)S(1)}, u32[]{:S(2)}, u32[]{:S(2)}) collective-permute-start(f32[64,1,128]{2,1,0:T(1,128)S(1)} %get-tuple-element.44), channel_id=1, source_target_pairs={{16,0},{32,16},{48,32},{64,48},{80,64},{96,80},{112,96},{17,1},{33... | collective-permute-start | bytes 98312 | tf_op jit(solution)/shard_map/ppermute | solution.py:24
  317.0 20.1 %collective-permute-start.6 = (f32[64,2,1]{2,1,0:T(2,128)S(1)}, f32[64,2,1]{2,1,0:T(2,128)S(1)}, u32[]{:S(2)}, u32[]{:S(2)}) collective-permute-start(f32[64,2,1]{2,1,0:T(2,128)S(1)} %bitcast.287), channel_id=1, source_target_pairs={{1,0},{2,1},{3,2},{4,3},{5,4},{6,5},{7,6},{8,7},{9,8},{10,9},{11,1... | collective-permute-start | bytes 1544 | tf_op jit(solution)/shard_map/ppermute | solution.py:24
  326.9 21.1 %collective-permute-start.5 = (f32[64,1,128]{2,1,0:T(1,128)S(1)}, f32[64,1,128]{2,1,0:T(1,128)S(1)}, u32[]{:S(2)}, u32[]{:S(2)}) collective-permute-start(f32[64,1,128]{2,1,0:T(1,128)S(1)} %bitcast.340), channel_id=1, source_target_pairs={{0,16},{16,32},{32,48},{48,64},{64,80},{80,96},{96,112},{1,17},{17... | collective-permute-start | bytes 98312 | tf_op jit(solution)/shard_map/ppermute | solution.py:21
  333.6 14.3 %collective-permute-start.7 = (f32[64,2,1]{2,1,0:T(2,128)S(1)}, f32[64,2,1]{2,1,0:T(2,128)S(1)}, u32[]{:S(2)}, u32[]{:S(2)}) collective-permute-start(f32[64,2,1]{2,1,0:T(2,128)S(1)} %copy.115), channel_id=1, source_target_pairs={{0,1},{1,2},{2,3},{3,4},{4,5},{5,6},{6,7},{7,8},{8,9},{9,10},{10,1... | collective-permute-start | bytes 1544 | tf_op jit(solution)/shard_map/ppermute | solution.py:21
  481.2 8.6 %copy-start.4 = (f32[64,64,2,128]{3,2,1,0:T(2,128)S(1)}, f32[64,64,2,128]{3,2,1,0:T(2,128)}, u32[]{:S(2)}) copy-start(f32[64,64,2,128]{3,2,1,0:T(2,128)} %param.23) | copy-start | bytes 12582916
  492.4 27.1 %collective-permute-start.8 = (f32[64,1,128]{2,1,0:T(1,128)S(1)}, f32[64,1,128]{2,1,0:T(1,128)S(1)}, u32[]{:S(2)}, u32[]{:S(2)}) collective-permute-start(f32[64,1,128]{2,1,0:T(1,128)S(1)} %get-tuple-element.40), channel_id=1, source_target_pairs={{16,0},{32,16},{48,32},{64,48},{80,64},{96,80},{112,96},{17,1},{33... | collective-permute-start | bytes 98312 | tf_op jit(solution)/shard_map/ppermute | solution.py:24
  493.7 20.1 %collective-permute-start.10 = (f32[64,2,1]{2,1,0:T(2,128)S(1)}, f32[64,2,1]{2,1,0:T(2,128)S(1)}, u32[]{:S(2)}, u32[]{:S(2)}) collective-permute-start(f32[64,2,1]{2,1,0:T(2,128)S(1)} %bitcast.299), channel_id=1, source_target_pairs={{1,0},{2,1},{3,2},{4,3},{5,4},{6,5},{7,6},{8,7},{9,8},{10,9},{11,1... | collective-permute-start | bytes 1544 | tf_op jit(solution)/shard_map/ppermute | solution.py:24
  503.6 21.3 %collective-permute-start.9 = (f32[64,1,128]{2,1,0:T(1,128)S(1)}, f32[64,1,128]{2,1,0:T(1,128)S(1)}, u32[]{:S(2)}, u32[]{:S(2)}) collective-permute-start(f32[64,1,128]{2,1,0:T(1,128)S(1)} %bitcast.339), channel_id=1, source_target_pairs={{0,16},{16,32},{32,48},{48,64},{64,80},{80,96},{96,112},{1,17},{17... | collective-permute-start | bytes 98312 | tf_op jit(solution)/shard_map/ppermute | solution.py:21
  510.3 14.5 %collective-permute-start.11 = (f32[64,2,1]{2,1,0:T(2,128)S(1)}, f32[64,2,1]{2,1,0:T(2,128)S(1)}, u32[]{:S(2)}, u32[]{:S(2)}) collective-permute-start(f32[64,2,1]{2,1,0:T(2,128)S(1)} %copy.125), channel_id=1, source_target_pairs={{0,1},{1,2},{2,3},{3,4},{4,5},{5,6},{6,7},{7,8},{8,9},{9,10},{10,1... | collective-permute-start | bytes 1544 | tf_op jit(solution)/shard_map/ppermute | solution.py:21
  514.9 79.4 %copy-start.1 = (bf16[1,1,16384,64]{2,3,1,0:T(8,128)(2,1)S(1)}, bf16[1,1,16384,64]{2,3,1,0:T(8,128)(2,1)}, u32[]{:S(2)}) copy-start(bf16[1,1,16384,64]{2,3,1,0:T(8,128)(2,1)} %param.18) | copy-start | bytes 6291460
where the time goes:
time: 604 us; the launch traced here: 595 us
  blocking collectives  322 us (53%)
  other arithmetic  97.1 us (16%)
  starting transfers between devices  51.7 us (9%)
  matrix products  45.6 us (8%)
  waiting for transfers between devices  42.9 us (7%)
  local copies, waits for them, and re-layouts  27.1 us (4%)
  between operations  8.77 us (1%)
    psum x3, blocking collectives, residual_norm(): return lax.psum(jnp.sum(residual * precond), ('sx', 'sy'))  190 us
    psum x2, blocking collectives, local(): step_size = rho_now / lax.psum(jnp.sum(direction * result), ('sx', 'sy'))  132 us
    dot_general x12, other arithmetic, apply_tiles(): return jnp.einsum('ijab,jab->iab', tile_set, vector, precision=HIGHEST)  51.5 us
    all_to_all x1, waiting for transfers between devices, local(): lax.all_to_all(produced, ('sx', 'sy'), split_axis=0, concat_axis=0, tiled...  42.9 us
    ppermute x6, starting transfers between devices, with_halo(): lax.ppermute(lax.slice_in_dim(block, block.shape[dim] - width, None, axis...  27.4 us
    dot_general x3, other arithmetic, apply_transposed(): return jnp.einsum('jiab,jab->iab', tile_set, vector, precision=HIGHEST)  24.9 us
    dot_general x1, matrix products, constitutive(): jnp.dot(hidden_one, w_second, preferred_element_type=jnp.float32)  22.2 us
    dot_general x1, matrix products, constitutive(): output = jnp.dot(hidden_two, w_third, preferred_element_type=jnp.float32)  17.9 us
  transfers between devices with their start and end apart: 13, of which 1 were waited for; matrix products, arithmetic and copies ran while one was open for 14% of the time, Pallas kernels for 0%

commit v1 on v0

v1 whole, which is shorter than its diff:
```python
import functools

import jax
import jax.numpy as jnp
from jax import lax
from jax.experimental import pallas as pl
from jax.experimental.pallas import tpu as pltpu
from jax.sharding import PartitionSpec as P

BLOCK_DOFS = 64
FEATURES = 64
ITERS = 3
PER_BLOCK = 64
DIAG_SHIFT = 5.0
MESH = pl.DeviceIdType.MESH
F32 = jnp.float32
BF16 = jnp.bfloat16
EVEN = pl.ds(0, 64, stride=2)
ODD = pl.ds(1, 64, stride=2)


def constitutive(features, w_first, w_second, w_third):
    hidden_one = jax.nn.silu(jnp.dot(features, w_first, preferred_element_type=F32)).astype(BF16)
    hidden_two = jax.nn.silu(jnp.dot(hidden_one, w_second, preferred_element_type=F32)).astype(BF16)
    output = jnp.dot(hidden_two, w_third, preferred_element_type=F32)
    stress = output[:, :BLOCK_DOFS]
    tangent = jax.nn.softplus(output[:, BLOCK_DOFS:]) / PER_BLOCK
    return jnp.concatenate([stress, tangent], axis=1).astype(BF16)


def permute(value, matrix, transposed):
    rows = value.shape[0]
    high = value.astype(BF16)
    rest = value - high.astype(F32)
    middle = rest.astype(BF16)
    low = (rest - middle.astype(F32)).astype(BF16)
    parts = jnp.concatenate([high, middle, low], axis=0)
    dims = (((1,), (1 if transposed else 0,)), ((), ()))
    product = lax.dot_general(parts, matrix, dims, preferred_element_type=F32)
    return product[:rows] + product[rows : 2 * rows] + product[2 * rows :]


def swap_pairs(row, swap):
    lane = lax.broadcasted_iota(jnp.int32, row.shape, 1)
    swapped = jnp.where(lane % 2 == 0, pltpu.roll(row, 127, 1), pltpu.roll(row, 1, 1))
    return jnp.where(swap > 0, swapped, row)


def column(row):
    return jnp.broadcast_to(row[0:1], (128, 128)).T


def cg_kernel(
    n_sx,
    n_sy,
    rows_hbm,
    owner_ref,
    diag_hbm,
    x_hbm,
    y_hbm,
    p_hbm,
    cols_ref,
    xmap_ref,
    yswap_ref,
    adjoint_ref,
    residual_ref,
    rows_ref,
    e_ref,
    x_ref,
    y_ref,
    p_ref,
    mp_ref,
    mx_ref,
    diag_ref,
    jac_ref,
    z_ref,
    d_ref,
    s_ref,
    vb_ref,
    red_ref,
    acc_ref,
    tmp_ref,
    part_p_ref,
    hx_out,
    hy_out,
    ix_out,
    iy_out,
    hx_in,
    hy_in,
    ix_in,
    iy_in,
    sum_y,
    sum_x,
    local_sem,
    halo_send,
    halo_recv,
    sum_send,
    sum_recv,
):
    i = lax.axis_index("sx")
    j = lax.axis_index("sy")
    loads = [
        pltpu.make_async_copy(src, dst, local_sem.at[k])
        for k, (src, dst) in enumerate(
            [(rows_hbm, rows_ref), (diag_hbm, e_ref), (x_hbm, x_ref), (y_hbm, y_ref), (p_hbm, p_ref)]
        )
    ]
    for load in loads:
        load.start()
    barrier = pltpu.get_barrier_semaphore()
    for k in range(1, n_sx):
        pl.semaphore_signal(barrier, inc=1, device_id=(lax.rem(i + k, n_sx), j), device_id_type=MESH)
    for k in range(1, n_sy):
        pl.semaphore_signal(barrier, inc=1, device_id=(i, lax.rem(j + k, n_sy)), device_id_type=MESH)
    pl.semaphore_wait(barrier, n_sx + n_sy - 2)

    def send(src, dst, slot, to):
        copy = pltpu.make_async_remote_copy(
            src_ref=src,
            dst_ref=dst,
            send_sem=halo_send.at[slot],
            recv_sem=halo_recv.at[slot],
            device_id=to,
            device_id_type=MESH,
        )
        copy.start()
        return copy

    x_next, x_prev = (lax.rem(i + 1, n_sx), j), (lax.rem(i + n_sx - 1, n_sx), j)
    y_next, y_prev = (i, lax.rem(j + 1, n_sy)), (i, lax.rem(j + n_sy - 1, n_sy))

    mp_ref[...] = (lax.broadcasted_iota(jnp.int32, (256, 256), 0) == cols_ref[0:1]).astype(F32).astype(BF16)
    mx_ref[...] = (lax.broadcasted_iota(jnp.int32, (128, 128), 0) == xmap_ref[0:1]).astype(F32).astype(BF16)
    yswap = yswap_ref[...]

    loads[0].wait()

    def assemble(step, total):
        owners = owner_ref[pl.ds(pl.multiple_of(step * 8, 8), 8), :]
        block = lax.broadcasted_iota(jnp.int32, (256, 128), 0)
        onehot = jnp.concatenate(
            [(block == owners[e : e + 1]).astype(F32).astype(BF16) for e in range(8)], axis=1
        )
        rows = rows_ref[pl.ds(pl.multiple_of(step * 1024, 1024), 1024), :]
        return total + jnp.dot(onehot, rows, preferred_element_type=F32)

    fields = lax.fori_loop(0, 16, assemble, jnp.zeros((256, 128), F32)).T
    residual_ref[EVEN, :] = fields[:64, :128]
    residual_ref[ODD, :] = fields[:64, 128:]
    diag_ref[EVEN, :] = fields[64:, :128] + DIAG_SHIFT
    diag_ref[ODD, :] = fields[64:, 128:] + DIAG_SHIFT
    for load in loads[1:]:
        load.wait()
    for k in range(64):
        jac_ref[2 * k : 2 * k + 2, :] = e_ref[k, 2 * k : 2 * k + 2, :]
    jac_ref[...] = diag_ref[...] + 2.0 * jac_ref[...]

    def transposed_pass(tiles):
        def body(step, total):
            for u in range(2):
                k = step * 2 + u
                total = total + tiles[k].reshape(16, 8, 128) * vb_ref[k][None]
            return total

        return lax.fori_loop(0, 32, body, jnp.zeros((16, 8, 128), F32)).reshape(128, 128)

    def forward_pass(tiles, partner):
        partner = partner.reshape(16, 8, 128)

        def body(step, carry):
            for u in range(2):
                k = step * 2 + u
                red_ref[k] += jnp.sum(tiles[k].reshape(16, 8, 128) * partner, axis=0)
            return carry

        lax.fori_loop(0, 32, body, 0)

    def both_pass(tiles, partner, first):
        partner = partner.reshape(16, 8, 128)

        def body(step, total):
            for u in range(2):
                k = step * 2 + u
                tile = tiles[k].reshape(16, 8, 128)
                forward = jnp.sum(tile * partner, axis=0)
                red_ref[k] = forward if first else red_ref[k] + forward
                total = total + tile * vb_ref[k][None]
            return total

        return lax.fori_loop(0, 32, body, jnp.zeros((16, 8, 128), F32)).reshape(128, 128)

    def global_sum(it):
        copies = []
        for stage, (buffer, mine, count) in enumerate([(sum_y, j, n_sy), (sum_x, i, n_sx)]):
            for k in range(1, count):
                peer = lax.rem(mine + k, count)
                copy = pltpu.make_async_remote_copy(
                    src_ref=buffer.at[it, mine],
                    dst_ref=buffer.at[it, mine],
                    send_sem=sum_send.at[it, stage],
                    recv_sem=sum_recv.at[it, stage],
                    device_id=(i, peer) if stage == 0 else (peer, j),
                    device_id_type=MESH,
                )
                copy.start()
            others = pltpu.make_async_copy(
                buffer.at[it, pl.ds(0, count - 1)], buffer.at[it, pl.ds(0, count - 1)], sum_recv.at[it, stage]
            )
            others.wait()
            total = jnp.sum(buffer[it], axis=0)
            if stage == 0:
                sum_x[it, i] = total
            copies.append((buffer, count, it, stage))
        return jnp.sum(total, axis=1, keepdims=True), copies

    lane = lax.broadcasted_iota(jnp.int32, (128, 128), 1)
    edge_x = jnp.where(i == n_sx - 1, 0.0, 1.0)
    edge_y = jnp.where(j == n_sy - 1, 0.0, 1.0)
    start_x = jnp.where(i == 0, 0.0, 1.0)
    start_y = jnp.where(j == 0, 0.0, 1.0)
    sent = []
    summed = []
    alpha = gamma_old = None
    for it in range(ITERS):
        residual = residual_ref[...]
        z = residual / jac_ref[...]
        z_ref[...] = z
        z_even, z_odd = z_ref[EVEN, :], z_ref[ODD, :]
        hx_out[it] = z_even
        hx = send(hx_out.at[it], hx_in.at[it], 4 * it, x_prev)
        hy_out[it] = z.T[0:8]
        hy = send(hy_out.at[it], hy_in.at[it], 4 * it + 1, y_prev)
        for q in range(4):
            vb_ref[:, 2 * q, :] = z_even
            vb_ref[:, 2 * q + 1, :] = z_odd
        tmp_ref[...] = transposed_pass(x_ref)
        ix_out[it] = permute(tmp_ref[ODD, :], mx_ref[...], True)
        ix = send(ix_out.at[it], ix_in.at[it], 4 * it + 2, x_next)
        turned = transposed_pass(y_ref)
        iy_out[it] = swap_pairs(turned.T[120:128], yswap)
        iy = send(iy_out.at[it], iy_in.at[it], 4 * it + 3, y_next)
        acc_ref[...] = diag_ref[...] * z + jnp.where(lane == 0, 0.0, pltpu.roll(turned, 1, 1))
        acc_ref[ODD, :] += tmp_ref[EVEN, :]
        acc_ref[...] += both_pass(e_ref, z, True)
        flat = permute(jnp.concatenate([z_even, z_odd], axis=1), mp_ref[...], False)
        part_p_ref[EVEN, :] = flat[:, :128]
        part_p_ref[ODD, :] = flat[:, 128:]
        tmp_ref[...] = both_pass(p_ref, part_p_ref[...], False)
        flat = permute(jnp.concatenate([tmp_ref[EVEN, :], tmp_ref[ODD, :]], axis=1), mp_ref[...], True)
        acc_ref[EVEN, :] += flat[:, :128]
        acc_ref[ODD, :] += flat[:, 128:]
        hx.wait_recv()
        tmp_ref[EVEN, :] = z_odd
        tmp_ref[ODD, :] = permute(hx_in[it], mx_ref[...], False) * edge_x
        forward_pass(x_ref, tmp_ref[...])
        hy.wait_recv()
        beyond = column(swap_pairs(hy_in[it], yswap)) * edge_y
        forward_pass(y_ref, jnp.where(lane == 127, beyond, pltpu.roll(z, 127, 1)))
        for a, part in ((0, EVEN), (1, ODD)):
            total = red_ref[:, a, :]
            for q in range(1, 4):
                total = total + red_ref[:, 2 * q + a, :]
            acc_ref[part, :] += total
        ix.wait_recv()
        acc_ref[EVEN, :] += ix_in[it] * start_x
        iy.wait_recv()
        acc_ref[...] += jnp.where(lane == 0, column(iy_in[it, 7:8]) * start_y, 0.0)
        sent += [hx, hy, ix, iy]
        applied = acc_ref[...]
        sums = jnp.concatenate(
            [
                jnp.sum(residual * z, axis=0, keepdims=True),
                jnp.sum(z * applied, axis=0, keepdims=True),
                jnp.zeros((6, 128), F32),
            ],
            axis=0,
        )
        sum_y[it, j] = sums
        totals, copies = global_sum(it)
        summed += copies
        gamma, delta = totals[0:1], totals[1:2]
        if it == 0:
            alpha = gamma / delta
            direction, image = z, applied
            adjoint_ref[...] = alpha * direction
        else:
            beta = gamma / gamma_old
            alpha = gamma / (delta - beta * gamma / alpha)
            direction = z + beta * d_ref[...]
            image = applied + beta * s_ref[...]
            adjoint_ref[...] += alpha * direction
        gamma_old = gamma
        residual_ref[...] = residual - alpha * image
        if it + 1 < ITERS:
            d_ref[...] = direction
            s_ref[...] = image
    for copy in sent:
        copy.wait_send()
    for buffer, count, it, stage in summed:
        pltpu.make_async_copy(
            buffer.at[it, pl.ds(0, count - 1)], buffer.at[it, pl.ds(0, count - 1)], sum_send.at[it, stage]
        ).wait()


def local(n_sx, n_sy, *args):
    (
        quad_features,
        w_first,
        w_second,
        w_third,
        quad_block,
        diag_tiles,
        x_tiles,
        y_tiles,
        p_tiles,
        tile_cols,
        x_map,
        y_map,
    ) = args
    sample_count = quad_features.shape[2]
    devices = n_sx * n_sy
    slots = sample_count // devices
    features = quad_features.reshape(sample_count, FEATURES)
    produced = constitutive(features, w_first, w_second, w_third).reshape(devices, slots, 2 * BLOCK_DOFS)
    received = lax.all_to_all(produced, ("sx", "sy"), split_axis=0, concat_axis=0, tiled=True)
    received = received.reshape(sample_count, 2 * BLOCK_DOFS)
    tiles = [t.reshape(64, 128, 128) for t in (diag_tiles, x_tiles, y_tiles, p_tiles)]
    owners = quad_block.reshape(128, 128)
    cols = jnp.broadcast_to(tile_cols.reshape(1, 256), (8, 256))
    xmap = jnp.broadcast_to(x_map.reshape(1, 128), (8, 128))
    yswap = jnp.broadcast_to(y_map[0, 0, 0], (8, 128))
    hbm = pl.BlockSpec(memory_space=pl.ANY)
    vmem = pl.BlockSpec(memory_space=pltpu.VMEM)
    square = pltpu.VMEM((128, 128), F32)
    adjoint, residual = pl.pallas_call(
        functools.partial(cg_kernel, n_sx, n_sy),
        out_shape=[jax.ShapeDtypeStruct((128, 128), F32)] * 2,
        in_specs=[hbm, vmem, hbm, hbm, hbm, hbm, vmem, vmem, vmem],
        out_specs=[vmem, vmem],
        scratch_shapes=[
            pltpu.VMEM((16384, 128), BF16),
            pltpu.VMEM((64, 128, 128), F32),
            pltpu.VMEM((64, 128, 128), F32),
            pltpu.VMEM((64, 128, 128), F32),
            pltpu.VMEM((64, 128, 128), F32),
            pltpu.VMEM((256, 256), BF16),
            pltpu.VMEM((128, 128), BF16),
            square,
            square,
            square,
            square,
            square,
            pltpu.VMEM((64, 8, 128), F32),
            pltpu.VMEM((64, 8, 128), F32),
            square,
            square,
            square,
            pltpu.VMEM((ITERS, 64, 128), F32),
            pltpu.VMEM((ITERS, 8, 128), F32),
            pltpu.VMEM((ITERS, 64, 128), F32),
            pltpu.VMEM((ITERS, 8, 128), F32),
            pltpu.VMEM((ITERS, 64, 128), F32),
            pltpu.VMEM((ITERS, 8, 128), F32),
            pltpu.VMEM((ITERS, 64, 128), F32),
            pltpu.VMEM((ITERS, 8, 128), F32),
            pltpu.VMEM((ITERS, n_sy, 8, 128), F32),
            pltpu.VMEM((ITERS, n_sx, 8, 128), F32),
            pltpu.SemaphoreType.DMA((5,)),
            pltpu.SemaphoreType.DMA((4 * ITERS,)),
            pltpu.SemaphoreType.DMA((4 * ITERS,)),
            pltpu.SemaphoreType.DMA((ITERS, 2)),
            pltpu.SemaphoreType.DMA((ITERS, 2)),
        ],
        compiler_params=pltpu.CompilerParams(
            collective_id=0, has_side_effects=True, vmem_limit_bytes=48 * 2**20
        ),
    )(received, owners, *tiles, cols, xmap, yswap)
    return adjoint.reshape(64, 2, 128), residual.reshape(64, 2, 128)


def solution(mesh):
    in_specs = (
        P("sx", "sy", None, None),
        P(),
        P(),
        P(),
        P("sx", "sy", None),
        P(None, None, "sx", "sy"),
        P(None, None, "sx", "sy"),
        P(None, None, "sx", "sy"),
        P(None, None, "sx", "sy"),
        P("sx", "sy", None),
        P("sx", "sy", None),
        P("sx", "sy", None),
    )
    out_specs = (P(None, "sx", "sy"), P(None, "sx", "sy"))
    return jax.shard_map(
        functools.partial(local, mesh.shape["sx"], mesh.shape["sy"]),
        mesh=mesh,
        in_specs=in_specs,
        out_specs=out_specs,
        check_vma=False,
    )
```

time: 604 us -> 183 us (0.30); the launches traced: 595 us -> 183 us
  blocking collectives: 322 us -> 64.3 us
  other arithmetic: 97.1 us -> 9.19 us
  Pallas kernels: 0 us -> 53.9 us
  starting transfers between devices: 51.7 us -> 0 us
  waiting for transfers between devices: 42.9 us -> 0 us
  local copies, waits for them, and re-layouts: 27.1 us -> 14.6 us
  between operations: 8.77 us -> 0.74 us
    psum x5 -> x0, blocking collectives: 322 us -> none  [the longest x3 190 us: residual_norm(): return lax.psum(jnp.sum(residual * precond), ('sx', 'sy'))]
    dot_general x15 -> x0, other arithmetic: 76.4 us -> none  [the longest x12 51.5 us: apply_tiles(): return jnp.einsum('ijab,jab->iab', tile_set, vector, precision=HIGHEST)]
    all_to_all x0 -> x1, blocking collectives: none -> 64.3 us  [local(): lax.all_to_all(produced, ('sx', 'sy'), split_axis=0, concat_axis=0, tiled...]
    pallas_call x0 -> x1, Pallas kernels: none -> 53.9 us  [local(): pl.pallas_call(functools.partial(cg_kernel, n_sx, n_sy), out_shape=[jax.S...]
    all_to_all x1 -> x0, waiting for transfers between devices: 42.9 us -> none  [local(): lax.all_to_all(produced, ('sx', 'sy'), split_axis=0, concat_axis=0, tiled...]
    ppermute x12 -> x0, starting transfers between devices: 39.4 us -> none  [the longest x6 27.4 us: with_halo(): lax.ppermute(lax.slice_in_dim(block, block.shape[dim] - width, None, axis...]
    gather x25 -> x0, local copies, waits for them, and re-layouts: 15 us -> none  [the longest x1 2.95 us: local(): jnp.diagonal(diag_tiles, axis1=0, axis2=1)]
    all_to_all x1 -> x0, starting transfers between devices: 12.4 us -> none  [local(): lax.all_to_all(produced, ('sx', 'sy'), split_axis=0, concat_axis=0, tiled...]
  transfers between devices with their start and end apart: 13 -> 0, of which waited for: 1 -> 0; matrix products, arithmetic and copies ran while one was open for 14% -> 0% of each run, Pallas kernels for 0% -> 0%
where the time goes in v1:
time: 183 us
  blocking collectives  64.3 us (35%)
  Pallas kernels  53.9 us (29%)
  matrix products  40.1 us (22%)
  local copies, waits for them, and re-layouts  14.6 us (8%)
  other arithmetic  9.19 us (5%)
    all_to_all x1, blocking collectives, local(): lax.all_to_all(produced, ('sx', 'sy'), split_axis=0, concat_axis=0, tiled...  64.3 us
    pallas_call x1, Pallas kernels, local(): pl.pallas_call(functools.partial(cg_kernel, n_sx, n_sy), out_shape=[jax.S...  53.9 us
    dot_general x1, matrix products, constitutive(): jnp.dot(hidden_one, w_second, preferred_element_type=F32)  22.2 us
    dot_general x1, matrix products, constitutive(): output = jnp.dot(hidden_two, w_third, preferred_element_type=F32)  17.9 us
    concatenate x2, local copies, waits for them, and re-layouts, constitutive(): return jnp.concatenate([stress, tangent], axis=1).astype(BF16)  7.94 us
    concatenate x1, other arithmetic, constitutive(): return jnp.concatenate([stress, tangent], axis=1).astype(BF16)  4.64 us
    another operation x1, other arithmetic  4.55 us
    slice x1, local copies, waits for them, and re-layouts, constitutive(): stress = output[:, :BLOCK_DOFS]  3.72 us

profile of v1, /device:TPU:1, one launch (start us, length us, event | category | flops | bytes accessed | tf_op | source)
XLA Modules:
  0.0 182.8 jit_solution(17799390086796632195)
XLA Ops:
  0.6 0.0 copy-start
  0.6 0.0 copy-start.6
  0.7 1.6 copy-done
  2.2 22.2 %fusion = f32[16384,512]{1,0:T(8,128)} fusion(bf16[512,512]{1,0:T(8,128)(2,1)} %param.14, bf16[64,512]{1,0:T(8,128)(2,1)} %param.13, bf16[1,1,16384,64]{2,3,1,0:T(8,128)(2,1)S(1)} %copy-done), kind=kOutput, calls=%fused_computation.2 | convolution fusion | flops 9705619456 | bytes 36241408 | tf_op jit(solution)/shard_map/dot_general | solution.py:24
  24.4 0.0 copy-done.6
  24.4 17.9 %fusion.1 = f32[16384,128]{0,1:T(8,128)} fusion(bf16[512,128]{1,0:T(8,128)(2,1)S(1)} %copy-done.6, f32[16384,512]{1,0:T(8,128)} %fusion), kind=kOutput, calls=%fused_computation.3 | convolution fusion | flops 2189426688 | bytes 42074112 | tf_op jit(solution)/shard_map/dot_general | solution.py:25
  42.4 3.7 %slice.17 = bf16[16384,64]{0,1:T(8,128)(2,1)} slice(f32[16384,128]{0,1:T(8,128)} %fusion.1), slice={[0:16384], [0:64]} | slice | bytes 4194304 | tf_op jit(solution)/shard_map/slice | solution.py:26
  46.1 4.6 %fusion.5 = bf16[16384,64]{0,1:T(8,128)(2,1)S(1)} fusion(f32[16384,128]{0,1:T(8,128)} %fusion.1), kind=kLoop, calls=%fused_computation.7 | loop fusion | flops 8388608 | bytes 6291456 | tf_op jit(solution)/shard_map/convert.2
  50.6 4.8 %copy.16 = bf16[16384,64]{1,0:T(8,128)(2,1)} copy(bf16[16384,64]{0,1:T(8,128)(2,1)} %slice.17) | data formatting | bytes 4194304 | tf_op jit(solution)/shard_map/concatenate | solution.py:28
  55.4 3.2 %copy.17 = bf16[16384,64]{1,0:T(8,128)(2,1)} copy(bf16[16384,64]{0,1:T(8,128)(2,1)S(1)} %fusion.5) | data formatting | bytes 4194304 | tf_op jit(solution)/shard_map/concatenate | solution.py:28
  58.6 4.6 %pad_maximum_fusion = bf16[128,128,128]{2,1,0:T(8,128)(2,1)S(1)} fusion(bf16[128,128,64]{2,1,0:T(8,128)(2,1)} %bitcast.26, bf16[128,128,64]{2,1,0:T(8,128)(2,1)} %bitcast.25), kind=kLoop, calls=%fused_computation.9 | loop fusion | flops 8388608 | bytes 8388608 | tf_op jit(solution)/shard_map/concatenate | solution.py:28
  63.2 0.0 copy-start.3
  63.2 0.0 copy-start.4
  63.3 0.0 copy-start.5
  63.3 0.0 copy-start.2
  63.3 64.3 %all_to_all.5 = bf16[128,128,128]{2,1,0:T(8,128)(2,1)S(1)} all-to-all(bf16[128,128,128]{2,1,0:T(8,128)(2,1)S(1)} %pad_maximum_fusion), channel_id=1, replica_groups=mesh['sx'=8,'sy'=16] {'sx','sy'}, dimensions={0} | all-to-all | bytes 8388608 | tf_op jit(solution)/shard_map/all_to_all | solution.py:325
  127.6 0.0 copy-done.3
  127.6 0.0 copy-done.4
  127.6 0.0 copy-done.5
  127.6 0.0 copy-done.2
  127.6 0.0 copy-start.1
  127.7 53.9 %shard_map.131 = (f32[128,128]{1,0:T(8,128)S(1)}, f32[128,128]{1,0:T(8,128)S(1)}) custom-call(bf16[16384,128]{1,0:T(8,128)(2,1)S(1)} %bitcast.21, s32[128,128]{1,0:T(8,128)S(1)} %bitcast.22, f32[64,128,128]{2,1,0:T(8,128)} %bitcast.27, f32[64,128,128]{2,1,0:T(8,128)} %bitcast.28, f32[64,128,128]{2,1,0:T(8,128)} %bitcast.29, f32[64,128,128]{2,1,0:T(8,128)} %bitcast.30, ...), custom_call_target="tpu_custom_call" | custom-call | tf_op jit(solution)/shard_map/pallas_call | solution.py:335
  181.5 0.6 copy.20
  182.2 0.6 copy.21
  182.8 0.0 copy-done.1
  (3 shorter events, 0.0 us)
Async XLA Ops:
  0.6 1.6 copy-start
  0.6 23.8 %copy-start.6 = (bf16[512,128]{1,0:T(8,128)(2,1)S(1)}, bf16[512,128]{1,0:T(8,128)(2,1)}, u32[]{:S(2)}) copy-start(bf16[512,128]{1,0:T(8,128)(2,1)} %param.15) | copy-start | bytes 393220
  63.2 64.3 %copy-start.3 = (s32[1,1,256]{2,1,0:T(1,128)S(1)}, s32[1,1,256]{2,1,0:T(1,128)}, u32[]{:S(2)}) copy-start(s32[1,1,256]{2,1,0:T(1,128)} %param.21) | copy-start | bytes 3076
  63.2 64.3 %copy-start.4 = (s32[1,1,128]{2,1,0:T(1,128)S(1)}, s32[1,1,128]{2,1,0:T(1,128)}, u32[]{:S(2)}) copy-start(s32[1,1,128]{2,1,0:T(1,128)} %param.22) | copy-start | bytes 1540
  63.3 64.3 %copy-start.5 = (s32[1,1,2]{2,1,0:T(1,128)S(1)}, s32[1,1,2]{2,1,0:T(1,128)}, u32[]{:S(2)}) copy-start(s32[1,1,2]{2,1,0:T(1,128)} %param.23) | copy-start | bytes 28
  63.3 64.4 %copy-start.2 = (s32[1,1,16384]{2,1,0:T(1,128)S(1)}, s32[1,1,16384]{2,1,0:T(1,128)}, u32[]{:S(2)}) copy-start(s32[1,1,16384]{2,1,0:T(1,128)} %param.16) | copy-start | bytes 196612
  127.6 55.1 %copy-start.1 = (bf16[1,1,16384,64]{2,3,1,0:T(8,128)(2,1)S(1)}, bf16[1,1,16384,64]{2,3,1,0:T(8,128)(2,1)}, u32[]{:S(2)}) copy-start(bf16[1,1,16384,64]{2,3,1,0:T(8,128)(2,1)} %param.12) | copy-start | bytes 6291460

commit v2 on v1

v2 whole, which is shorter than its diff:
```python
import functools

import jax
import jax.numpy as jnp
from jax import lax
from jax.experimental import pallas as pl
from jax.experimental.pallas import tpu as pltpu
from jax.sharding import PartitionSpec as P

FEATURES = 64
ITERS = 3
PER_BLOCK = 64
DIAG_SHIFT = 5.0
MESH = pl.DeviceIdType.MESH
F32 = jnp.float32
BF16 = jnp.bfloat16
EVEN = pl.ds(0, 64, stride=2)
ODD = pl.ds(1, 64, stride=2)


def permute(value, matrix, transposed):
    rows = value.shape[0]
    high = value.astype(BF16)
    rest = value - high.astype(F32)
    middle = rest.astype(BF16)
    low = (rest - middle.astype(F32)).astype(BF16)
    parts = jnp.concatenate([high, middle, low], axis=0)
    dims = (((1,), (1 if transposed else 0,)), ((), ()))
    product = lax.dot_general(parts, matrix, dims, preferred_element_type=F32)
    return product[:rows] + product[rows : 2 * rows] + product[2 * rows :]


def swap_pairs(row, swap):
    lane = lax.broadcasted_iota(jnp.int32, row.shape, 1)
    swapped = jnp.where(lane % 2 == 0, pltpu.roll(row, 127, 1), pltpu.roll(row, 1, 1))
    return jnp.where(swap > 0, swapped, row)


def column(row):
    return jnp.broadcast_to(row, (128, 128)).T


def silu_of_half(u):
    return (u + u * jnp.tanh(u)).astype(BF16)


def kernel(
    feat_hbm,
    w1_ref,
    w2_ref,
    w3_ref,
    owner_ref,
    diag_hbm,
    x_hbm,
    y_hbm,
    p_hbm,
    cols_ref,
    xmap_ref,
    yswap_ref,
    adjoint_ref,
    residual_ref,
    feat_ref,
    w1h_ref,
    w2h_ref,
    prod_ref,
    ring_ref,
    plane_out,
    plane_ref,
    index_out,
    index_ref,
    e_ref,
    x_ref,
    y_ref,
    p_ref,
    mp_ref,
    mx_ref,
    vectors,
    vb_ref,
    red_ref,
    acc_ref,
    tmp_ref,
    hx_out,
    hy_out,
    ix_out,
    iy_out,
    hx_in,
    hy_in,
    ix_in,
    iy_in,
    sum_a,
    sum_b,
    local_sem,
    ring_send,
    ring_recv,
    plane_sem,
    index_sem,
    halo_send,
    halo_recv,
    sum_send,
    sum_recv,
):
    i = lax.axis_index("sx")
    j = lax.axis_index("sy")
    y, zh = i // 2, lax.rem(i, 2)
    zl, jl = j // 8, lax.rem(j, 8)
    x, core = jl // 2, lax.rem(j, 2)

    loads = [
        pltpu.make_async_copy(src, dst, local_sem.at[k])
        for k, (src, dst) in enumerate(
            [(feat_hbm, feat_ref), (diag_hbm, e_ref), (x_hbm, x_ref), (y_hbm, y_ref), (p_hbm, p_ref)]
        )
    ]
    for load in loads:
        load.start()

    def pick(first, second):
        return first * (1 - core) + second * core

    others = [(i, lax.rem(j + k, 16)) for k in range(1, 16)]
    others += [(lax.rem(i + k, 8), j) for k in range(1, 8)]
    others += [(lax.rem(i + k, 8), lax.rem(j + 8, 16)) for k in range(1, 8)]
    others += [(lax.rem(y + k, 4) * 2 + zh, j + 1 - 2 * core) for k in range(1, 4)]
    others += [(y * 2 + 1 - zh, lax.rem(j + 2 * k, 16)) for k in range(1, 8)]
    barrier = pltpu.get_barrier_semaphore()
    for other in others:
        pl.semaphore_signal(barrier, inc=1, device_id=other, device_id_type=MESH)

    w1h_ref[...] = (w1_ref[...].astype(F32) * 0.5).astype(BF16)
    w2h_ref[...] = (w2_ref[...].astype(F32) * 0.5).astype(BF16)

    place = pick(i * 2 + zl, zh * 8 + zl * 4 + x)

    def plane_device(t):
        return pick(t // 2, y * 2 + t // 8), pick(lax.rem(t, 2) * 8 + x * 2, lax.rem(t, 8) * 2 + 1)

    for t in range(16):
        for q in range(4):
            first = pick((t // 2) * 16 + (t % 2) * 8 + q * 2, (q * 2 + t // 8) * 16 + (t % 8) * 2)
            index_out[t, 2 * q : 2 * q + 2, :] = owner_ref[pl.ds(first, 2), :]
    index_ref[place] = index_out[place]
    pl.semaphore_wait(barrier, len(others))

    def send_index(s, carry):
        t = lax.rem(place + s, 16)
        pltpu.make_async_remote_copy(
            src_ref=index_out.at[t],
            dst_ref=index_ref.at[place],
            send_sem=index_sem.at[0],
            recv_sem=index_sem.at[1],
            device_id=plane_device(t),
            device_id_type=MESH,
        ).start()
        return carry

    lax.fori_loop(1, 16, send_index, 0)

    mp_ref[...] = (lax.broadcasted_iota(jnp.int32, (256, 256), 0) == cols_ref[0:1]).astype(F32).astype(BF16)
    mx_ref[...] = (lax.broadcasted_iota(jnp.int32, (128, 128), 0) == xmap_ref[0:1]).astype(F32).astype(BF16)
    yswap = yswap_ref[...]

    loads[0].wait()
    lane512 = lax.broadcasted_iota(jnp.int32, (256, 128), 1)

    def chunk(c, carry):
        k, part = c // 4, lax.rem(c, 4)
        pair = k // 2
        turn = jnp.where(k >= 6, 0, jnp.where(pair == 2, 2, 1 + 2 * pair))
        other_class = jnp.where(k >= 6, 7 - k, lax.rem(k, 2))
        dcore = lax.rem(core + other_class, 2)
        dx = lax.rem(x + turn * (1 - dcore), 4)
        dy = lax.rem(y + turn * dcore, 4)
        for half in range(2):
            blocks = []
            for u in range(2):
                t = part * 4 + half * 2 + u
                ri = (1 - dcore) * (t // 2) + dcore * (dy * 2 + t // 8)
                rj = (1 - dcore) * (lax.rem(t, 2) * 8 + dx * 2) + dcore * (lax.rem(t, 8) * 2 + 1)
                start = pl.multiple_of((ri * 16 + rj) * 128, 128)
                blocks.append(feat_ref[pl.ds(start, 128), :])
            rows = jnp.concatenate(blocks, axis=0)
            hidden = silu_of_half(jnp.dot(rows, w1h_ref[...], preferred_element_type=F32))
            hidden = silu_of_half(jnp.dot(hidden, w2h_ref[...], preferred_element_type=F32))
            output = jnp.dot(hidden, w3_ref[...], preferred_element_type=F32)
            softplus = jnp.maximum(output, 0.0) + jnp.log(1.0 + jnp.exp(-jnp.abs(output)))
            output = jnp.where(lane512 < 64, output, softplus * (1.0 / PER_BLOCK)).astype(BF16)
            prod_ref[c, 2 * half : 2 * half + 2] = output.reshape(2, 128, 128)
        slot = (1 - dcore) * (x * 2 + core) + dcore * (y * 2 + core)

        @pl.when(k < 7)
        def _():
            pltpu.make_async_remote_copy(
                src_ref=prod_ref.at[c],
                dst_ref=ring_ref.at[slot, pl.ds(part * 4, 4)],
                send_sem=ring_send,
                recv_sem=ring_recv.at[slot],
                device_id=(dy * 2 + zh, (zl * 4 + dx) * 2 + dcore),
                device_id_type=MESH,
            ).start()

        @pl.when(k == 7)
        def _():
            ring_ref[slot, pl.ds(part * 4, 4)] = prod_ref[c]

        return carry

    lax.fori_loop(0, 32, chunk, 0)

    mine = pick(x * 2 + core, y * 2 + core)
    pltpu.make_async_copy(index_ref.at[pl.ds(0, 15)], index_ref.at[pl.ds(0, 15)], index_sem.at[1]).wait()
    for s in range(1, 8):
        slot = lax.rem(mine + s, 8)
        pltpu.make_async_copy(ring_ref.at[slot], ring_ref.at[slot], ring_recv.at[slot]).wait()

    def reduce_rows(s, carry):
        t = lax.rem(place + s, 16)
        owners = index_ref[t]
        block = lax.broadcasted_iota(jnp.int32, (256, 128), 0)
        onehot = jnp.concatenate(
            [(block == owners[e : e + 1]).astype(F32).astype(BF16) for e in range(8)], axis=1
        )
        rows = ring_ref[:, t].reshape(1024, 128)
        plane_out[t] = jnp.dot(onehot, rows, preferred_element_type=F32).astype(BF16)

        @pl.when(s < 16)
        def _():
            pltpu.make_async_remote_copy(
                src_ref=plane_out.at[t],
                dst_ref=plane_ref.at[place],
                send_sem=plane_sem.at[0],
                recv_sem=plane_sem.at[1],
                device_id=plane_device(t),
                device_id_type=MESH,
            ).start()

        @pl.when(s == 16)
        def _():
            plane_ref[place] = plane_out[t]

        return carry

    lax.fori_loop(1, 17, reduce_rows, 0)
    for load in loads[1:]:
        load.wait()
    jac_ref, diag_ref, u_ref, w_ref, d_ref, s_ref, q_ref, zz_ref = (vectors.at[k] for k in range(8))
    for k in range(64):
        jac_ref[2 * k : 2 * k + 2, :] = e_ref[k, 2 * k : 2 * k + 2, :]
    pltpu.make_async_copy(plane_ref.at[pl.ds(0, 15)], plane_ref.at[pl.ds(0, 15)], plane_sem.at[1]).wait()
    total = plane_ref[0].astype(F32)
    for t in range(1, 16):
        total = total + plane_ref[t].astype(F32)
    fields = total.T
    residual_ref[EVEN, :] = fields[:64, :128]
    residual_ref[ODD, :] = fields[:64, 128:]
    diag_ref[EVEN, :] = fields[64:, :128] + DIAG_SHIFT
    diag_ref[ODD, :] = fields[64:, 128:] + DIAG_SHIFT
    jac_ref[...] = diag_ref[...] + 2.0 * jac_ref[...]

    x_next, x_prev = (lax.rem(i + 1, 8), j), (lax.rem(i + 7, 8), j)
    y_next, y_prev = (i, lax.rem(j + 1, 16)), (i, lax.rem(j + 15, 16))
    lane = lax.broadcasted_iota(jnp.int32, (128, 128), 1)
    edge_x = jnp.where(i == 7, 0.0, 1.0)
    edge_y = jnp.where(j == 15, 0.0, 1.0)
    start_x = jnp.where(i == 0, 0.0, 1.0)
    start_y = jnp.where(j == 0, 0.0, 1.0)

    def send(src, dst, slot, to):
        copy = pltpu.make_async_remote_copy(
            src_ref=src,
            dst_ref=dst,
            send_sem=halo_send.at[slot],
            recv_sem=halo_recv.at[slot],
            device_id=to,
            device_id_type=MESH,
        )
        copy.start()
        return copy

    def transposed_pass(tiles):
        def body(step, total):
            for u in range(2):
                k = step * 2 + u
                total = total + tiles[k].reshape(16, 8, 128) * vb_ref[k][None]
            return total

        return lax.fori_loop(0, 32, body, jnp.zeros((16, 8, 128), F32)).reshape(128, 128)

    def forward_pass(tiles, partner):
        partner = partner.reshape(16, 8, 128)

        def body(step, carry):
            for u in range(2):
                k = step * 2 + u
                red_ref[k] += jnp.sum(tiles[k].reshape(16, 8, 128) * partner, axis=0)
            return carry

        lax.fori_loop(0, 32, body, 0)

    def both_pass(tiles, partner, first):
        partner = partner.reshape(16, 8, 128)

        def body(step, total):
            for u in range(2):
                k = step * 2 + u
                tile = tiles[k].reshape(16, 8, 128)
                forward = jnp.sum(tile * partner, axis=0)
                red_ref[k] = forward if first else red_ref[k] + forward
                total = total + tile * vb_ref[k][None]
            return total

        return lax.fori_loop(0, 32, body, jnp.zeros((16, 8, 128), F32)).reshape(128, 128)

    index_b = i * 2 + zl

    def sum_begin(it, first, second):
        sum_a[it, jl] = jnp.concatenate(
            [jnp.sum(first, axis=0, keepdims=True), jnp.sum(second, axis=0, keepdims=True)], axis=0
        )
        for k in range(1, 8):
            pltpu.make_async_remote_copy(
                src_ref=sum_a.at[it, jl],
                dst_ref=sum_a.at[it, jl],
                send_sem=sum_send.at[it, 0],
                recv_sem=sum_recv.at[it, 0],
                device_id=(i, zl * 8 + lax.rem(jl + k, 8)),
                device_id_type=MESH,
            ).start()

    def sum_middle(it):
        pltpu.make_async_copy(sum_a.at[it, pl.ds(0, 7)], sum_a.at[it, pl.ds(0, 7)], sum_recv.at[it, 0]).wait()
        sum_b[it, index_b] = jnp.sum(sum_a[it], axis=0)
        for k in range(1, 16):
            peer = lax.rem(index_b + k, 16)
            pltpu.make_async_remote_copy(
                src_ref=sum_b.at[it, index_b],
                dst_ref=sum_b.at[it, index_b],
                send_sem=sum_send.at[it, 1],
                recv_sem=sum_recv.at[it, 1],
                device_id=(peer // 2, lax.rem(peer, 2) * 8 + jl),
                device_id_type=MESH,
            ).start()

    def sum_end(it):
        pltpu.make_async_copy(sum_b.at[it, pl.ds(0, 15)], sum_b.at[it, pl.ds(0, 15)], sum_recv.at[it, 1]).wait()
        total = jnp.sum(jnp.sum(sum_b[it], axis=0), axis=1, keepdims=True)
        return total[0:1], total[1:2]

    sent = []

    def apply(it, z, between):
        tmp_ref[...] = z
        z_even, z_odd = tmp_ref[EVEN, :], tmp_ref[ODD, :]
        hx_out[it] = z_even
        hx = send(hx_out.at[it], hx_in.at[it], 4 * it, x_prev)
        hy_out[it] = z.T[0:8]
        hy = send(hy_out.at[it], hy_in.at[it], 4 * it + 1, y_prev)
        for q in range(4):
            vb_ref[:, 2 * q, :] = z_even
            vb_ref[:, 2 * q + 1, :] = z_odd
        tmp_ref[...] = transposed_pass(x_ref)
        ix_out[it] = permute(tmp_ref[ODD, :], mx_ref[...], True)
        ix = send(ix_out.at[it], ix_in.at[it], 4 * it + 2, x_next)
        turned = transposed_pass(y_ref)
        iy_out[it] = swap_pairs(turned.T[120:128], yswap)
        iy = send(iy_out.at[it], iy_in.at[it], 4 * it + 3, y_next)
        acc_ref[...] = diag_ref[...] * z + jnp.where(lane == 0, 0.0, pltpu.roll(turned, 1, 1))
        acc_ref[ODD, :] += tmp_ref[EVEN, :]
        between()
        acc_ref[...] += both_pass(e_ref, z, True)
        flat = permute(jnp.concatenate([z_even, z_odd], axis=1), mp_ref[...], False)
        tmp_ref[EVEN, :] = flat[:, :128]
        tmp_ref[ODD, :] = flat[:, 128:]
        tmp_ref[...] = both_pass(p_ref, tmp_ref[...], False)
        flat = permute(jnp.concatenate([tmp_ref[EVEN, :], tmp_ref[ODD, :]], axis=1), mp_ref[...], True)
        acc_ref[EVEN, :] += flat[:, :128]
        acc_ref[ODD, :] += flat[:, 128:]
        hx.wait_recv()
        tmp_ref[EVEN, :] = z_odd
        tmp_ref[ODD, :] = permute(hx_in[it], mx_ref[...], False) * edge_x
        forward_pass(x_ref, tmp_ref[...])
        hy.wait_recv()
        beyond = column(swap_pairs(hy_in[it], yswap)[0:1]) * edge_y
        forward_pass(y_ref, jnp.where(lane == 127, beyond, pltpu.roll(z, 127, 1)))
        for a, part in ((0, EVEN), (1, ODD)):
            total = red_ref[:, a, :]
            for q in range(1, 4):
                total = total + red_ref[:, 2 * q + a, :]
            acc_ref[part, :] += total
        ix.wait_recv()
        acc_ref[EVEN, :] += ix_in[it] * start_x
        iy.wait_recv()
        acc_ref[...] += jnp.where(lane == 0, column(iy_in[it, 7:8]) * start_y, 0.0)
        sent.extend([hx, hy, ix, iy])
        return acc_ref[...]

    u_ref[...] = residual_ref[...] / jac_ref[...]
    w_ref[...] = apply(0, u_ref[...], lambda: None)
    alpha = gamma_old = None
    for it in range(ITERS):
        last = it + 1 == ITERS
        sum_begin(it, residual_ref[...] * u_ref[...], w_ref[...] * u_ref[...])
        if last:
            sum_middle(it)
        else:
            m = w_ref[...] / jac_ref[...]
            n = apply(it + 1, m, functools.partial(sum_middle, it))
        gamma, delta = sum_end(it)
        if it == 0:
            alpha = gamma / delta
            direction, image = u_ref[...], w_ref[...]
            adjoint_ref[...] = alpha * direction
        else:
            beta = gamma / gamma_old
            alpha = gamma / (delta - beta * gamma / alpha)
            direction = u_ref[...] + beta * d_ref[...]
            image = w_ref[...] + beta * s_ref[...]
            adjoint_ref[...] += alpha * direction
            if not last:
                m = m + beta * q_ref[...]
                n = n + beta * zz_ref[...]
        gamma_old = gamma
        residual_ref[...] -= alpha * image
        if not last:
            d_ref[...] = direction
            s_ref[...] = image
            q_ref[...] = m
            zz_ref[...] = n
            u_ref[...] -= alpha * m
            w_ref[...] -= alpha * n

    for copy in sent:
        copy.wait_send()
    for it in range(ITERS):
        for stage, (buffer, count) in enumerate([(sum_a, 7), (sum_b, 15)]):
            mover = buffer.at[it, pl.ds(0, count)]
            pltpu.make_async_copy(mover, mover, sum_send.at[it, stage]).wait()
    pltpu.make_async_copy(prod_ref.at[pl.ds(0, 28)], prod_ref.at[pl.ds(0, 28)], ring_send).wait()
    pltpu.make_async_copy(plane_ref.at[pl.ds(0, 15)], plane_ref.at[pl.ds(0, 15)], plane_sem.at[0]).wait()
    pltpu.make_async_copy(index_ref.at[pl.ds(0, 15)], index_ref.at[pl.ds(0, 15)], index_sem.at[0]).wait()


def local(*args):
    (
        quad_features,
        w_first,
        w_second,
        w_third,
        quad_block,
        diag_tiles,
        x_tiles,
        y_tiles,
        p_tiles,
        tile_cols,
        x_map,
        y_map,
    ) = args
    features = quad_features.reshape(16384, FEATURES)
    tiles = [t.reshape(64, 128, 128) for t in (diag_tiles, x_tiles, y_tiles, p_tiles)]
    owners = quad_block.reshape(128, 128)
    cols = jnp.broadcast_to(tile_cols.reshape(1, 256), (8, 256))
    xmap = jnp.broadcast_to(x_map.reshape(1, 128), (8, 128))
    yswap = jnp.broadcast_to(y_map[0, 0, 0], (8, 128))
    hbm = pl.BlockSpec(memory_space=pl.ANY)
    vmem = pl.BlockSpec(memory_space=pltpu.VMEM)
    square = pltpu.VMEM((128, 128), F32)
    tile = pltpu.VMEM((64, 128, 128), F32)
    halves = pltpu.VMEM((ITERS, 64, 128), F32)
    strip = pltpu.VMEM((ITERS, 8, 128), F32)
    dma = pltpu.SemaphoreType.DMA
    adjoint, residual = pl.pallas_call(
        kernel,
        out_shape=[jax.ShapeDtypeStruct((128, 128), F32)] * 2,
        in_specs=[hbm, vmem, vmem, vmem, vmem, hbm, hbm, hbm, hbm, vmem, vmem, vmem],
        out_specs=[vmem, vmem],
        scratch_shapes=[
            pltpu.VMEM((16384, FEATURES), BF16),
            pltpu.VMEM((64, 512), BF16),
            pltpu.VMEM((512, 512), BF16),
            pltpu.VMEM((32, 4, 128, 128), BF16),
            pltpu.VMEM((8, 16, 128, 128), BF16),
            pltpu.VMEM((16, 256, 128), BF16),
            pltpu.VMEM((16, 256, 128), BF16),
            pltpu.VMEM((16, 8, 128), jnp.int32),
            pltpu.VMEM((16, 8, 128), jnp.int32),
            tile,
            tile,
            tile,
            tile,
            pltpu.VMEM((256, 256), BF16),
            pltpu.VMEM((128, 128), BF16),
            pltpu.VMEM((8, 128, 128), F32),
            pltpu.VMEM((64, 8, 128), F32),
            pltpu.VMEM((64, 8, 128), F32),
            square,
            square,
            halves,
            strip,
            halves,
            strip,
            halves,
            strip,
            halves,
            strip,
            pltpu.VMEM((ITERS, 8, 2, 128), F32),
            pltpu.VMEM((ITERS, 16, 2, 128), F32),
            dma((5,)),
            dma,
            dma((8,)),
            dma((2,)),
            dma((2,)),
            dma((4 * ITERS,)),
            dma((4 * ITERS,)),
            dma((ITERS, 2)),
            dma((ITERS, 2)),
        ],
        compiler_params=pltpu.CompilerParams(
            collective_id=0, has_side_effects=True, vmem_limit_bytes=56 * 2**20
        ),
    )(features, w_first, w_second, w_third, owners, *tiles, cols, xmap, yswap)
    return adjoint.reshape(64, 2, 128), residual.reshape(64, 2, 128)


def solution(mesh):
    in_specs = (
        P("sx", "sy", None, None),
        P(),
        P(),
        P(),
        P("sx", "sy", None),
        P(None, None, "sx", "sy"),
        P(None, None, "sx", "sy"),
        P(None, None, "sx", "sy"),
        P(None, None, "sx", "sy"),
        P("sx", "sy", None),
        P("sx", "sy", None),
        P("sx", "sy", None),
    )
    out_specs = (P(None, "sx", "sy"), P(None, "sx", "sy"))
    return jax.shard_map(local, mesh=mesh, in_specs=in_specs, out_specs=out_specs, check_vma=False)
```

time: 183 us -> 104 us (0.57)
  blocking collectives: 64.3 us -> 0 us
  matrix products: 40.1 us -> 0 us
  Pallas kernels: 53.9 us -> 91.7 us
  other arithmetic: 9.19 us -> 0 us
  local copies, waits for them, and re-layouts: 14.6 us -> 11.5 us
    all_to_all x1 -> x0, blocking collectives: 64.3 us -> none  [local(): lax.all_to_all(produced, ('sx', 'sy'), split_axis=0, concat_axis=0, tiled...]
    dot_general x2 -> x0, matrix products: 40.1 us -> none  [the longest x1 22.2 us: constitutive(): jnp.dot(hidden_one, w_second, preferred_element_type=F32)]
    pallas_call x1, Pallas kernels: 53.9 us -> 91.7 us  [local(): pl.pallas_call(kernel, out_shape=[jax.ShapeDtypeStruct((128, 128), F32)]...]
    concatenate x2 -> x0, local copies, waits for them, and re-layouts: 7.94 us -> none  [constitutive(): return jnp.concatenate([stress, tangent], axis=1).astype(BF16)]
    unnamed x16 -> x3, local copies, waits for them, and re-layouts: 2.88 us -> 7.73 us
    concatenate x1 -> x0, other arithmetic: 4.64 us -> none  [constitutive(): return jnp.concatenate([stress, tangent], axis=1).astype(BF16)]
    another operation x1 -> x0, other arithmetic: 4.55 us -> none
    slice x1 -> x0, local copies, waits for them, and re-layouts: 3.72 us -> none  [constitutive(): stress = output[:, :BLOCK_DOFS]]
where the time goes in v2:
time: 104 us
  Pallas kernels  91.7 us (88%)
  local copies, waits for them, and re-layouts  11.5 us (11%)
    pallas_call x1, Pallas kernels, local(): pl.pallas_call(kernel, out_shape=[jax.ShapeDtypeStruct((128, 128), F32)]...  91.7 us
    unnamed x3, local copies, waits for them, and re-layouts  7.73 us

profile of v2, /device:TPU:1, one launch (start us, length us, event | category | flops | bytes accessed | tf_op | source)
XLA Modules:
  0.0 103.9 jit_solution(7158622889999447491)
XLA Ops:
  0.6 1.2 %broadcast_in_dim.20.xmap_ref = s32[8,128]{1,0:T(8,128)} broadcast(s32[128]{0:T(128)} %bitcast.21), dimensions={1} | broadcast | bytes 4608 | tf_op jit(solution)/shard_map/broadcast_in_dim | solution.py:461
  1.9 1.2 %broadcast_in_dim.21.yswap_ref = s32[8,128]{1,0:T(8,128)} broadcast(s32[]{:T(128)} %bitcast.22), dimensions={} | broadcast | bytes 4100 | tf_op jit(solution)/shard_map/broadcast_in_dim | solution.py:462
  3.1 1.3 %broadcast_in_dim.18.cols_ref = s32[8,256]{1,0:T(8,128)} broadcast(s32[256]{0:T(256)} %bitcast.20), dimensions={1} | broadcast | bytes 9216 | tf_op jit(solution)/shard_map/broadcast_in_dim | solution.py:460
  4.4 4.8 %copy.14 = bf16[1,1,16384,64]{3,2,1,0:T(8,128)(2,1)} copy(bf16[1,1,16384,64]{2,3,1,0:T(8,128)(2,1)} %param.12) | data formatting | bytes 4194304 | tf_op args[0]
  9.2 91.7 %shard_map.131 = (f32[128,128]{1,0:T(8,128)}, f32[128,128]{1,0:T(8,128)}) custom-call(bf16[16384,64]{1,0:T(8,128)(2,1)} %bitcast.12, bf16[64,512]{1,0:T(8,128)(2,1)} %w1_ref.1, bf16[512,512]{1,0:T(8,128)(2,1)} %w2_ref.1, bf16[512,128]{1,0:T(8,128)(2,1)} %w3_ref.1, s32[128,128]{1,0:T(8,128)} %bitcast.17, f32[64,128,128]{2,1,0:T(8,128)} %bitcast.13, ...), custom_call_target="tpu_custom_call" | custom-call | tf_op jit(solution)/shard_map/pallas_call | solution.py:470
  100.9 1.5 %copy.17 = f32[64,2,128]{2,1,0:T(2,128)} copy(f32[64,2,128]{2,1,0:T(2,128)} %bitcast.19) | data formatting | bytes 131072
  102.4 1.5 %copy.18 = f32[64,2,128]{2,1,0:T(2,128)} copy(f32[64,2,128]{2,1,0:T(2,128)} %bitcast.18) | data formatting | bytes 131072

commit v3 on v2

--- a/solution.py
+++ b/solution.py
@@ -60,8 +60,9 @@
     adjoint_ref,
     residual_ref,
     feat_ref,
-    w1h_ref,
-    w2h_ref,
+    w1t_ref,
+    w2t_ref,
+    w3t_ref,
     prod_ref,
     ring_ref,
     plane_out,
@@ -126,10 +127,12 @@
     for other in others:
         pl.semaphore_signal(barrier, inc=1, device_id=other, device_id_type=MESH)
 
-    w1h_ref[...] = (w1_ref[...].astype(F32) * 0.5).astype(BF16)
-    w2h_ref[...] = (w2_ref[...].astype(F32) * 0.5).astype(BF16)
-
-    place = pick(i * 2 + zl, zh * 8 + zl * 4 + x)
+    w1t_ref[...] = (w1_ref[...].astype(F32) * 0.5).T.astype(BF16)
+    w2t_ref[...] = (w2_ref[...].astype(F32) * 0.5).T.astype(BF16)
+    w3t_ref[...] = w3_ref[...].astype(F32).T.astype(BF16)
+
+    place_yz, place_xz = i * 2 + zl, zh * 8 + zl * 4 + x
+    place = pick(place_yz, place_xz)
 
     def plane_device(t):
         return pick(t // 2, y * 2 + t // 8), pick(lax.rem(t, 2) * 8 + x * 2, lax.rem(t, 8) * 2 + 1)
@@ -139,7 +142,6 @@
             first = pick((t // 2) * 16 + (t % 2) * 8 + q * 2, (q * 2 + t // 8) * 16 + (t % 8) * 2)
             index_out[t, 2 * q : 2 * q + 2, :] = owner_ref[pl.ds(first, 2), :]
     index_ref[place] = index_out[place]
-    pl.semaphore_wait(barrier, len(others))
 
     def send_index(s, carry):
         t = lax.rem(place + s, 16)
@@ -153,93 +155,123 @@
         ).start()
         return carry
 
-    lax.fori_loop(1, 16, send_index, 0)
-
     mp_ref[...] = (lax.broadcasted_iota(jnp.int32, (256, 256), 0) == cols_ref[0:1]).astype(F32).astype(BF16)
     mx_ref[...] = (lax.broadcasted_iota(jnp.int32, (128, 128), 0) == xmap_ref[0:1]).astype(F32).astype(BF16)
-    yswap = yswap_ref[...]
+    yswap = yswap_ref[0:1, 0:1]
 
     loads[0].wait()
-    lane512 = lax.broadcasted_iota(jnp.int32, (256, 128), 1)
-
-    def chunk(c, carry):
-        k, part = c // 4, lax.rem(c, 4)
-        pair = k // 2
-        turn = jnp.where(k >= 6, 0, jnp.where(pair == 2, 2, 1 + 2 * pair))
-        other_class = jnp.where(k >= 6, 7 - k, lax.rem(k, 2))
-        dcore = lax.rem(core + other_class, 2)
-        dx = lax.rem(x + turn * (1 - dcore), 4)
-        dy = lax.rem(y + turn * dcore, 4)
+
+    def chunk(c, part):
         for half in range(2):
-            blocks = []
-            for u in range(2):
-                t = part * 4 + half * 2 + u
-                ri = (1 - dcore) * (t // 2) + dcore * (dy * 2 + t // 8)
-                rj = (1 - dcore) * (lax.rem(t, 2) * 8 + dx * 2) + dcore * (lax.rem(t, 8) * 2 + 1)
-                start = pl.multiple_of((ri * 16 + rj) * 128, 128)
-                blocks.append(feat_ref[pl.ds(start, 128), :])
-            rows = jnp.concatenate(blocks, axis=0)
-            hidden = silu_of_half(jnp.dot(rows, w1h_ref[...], preferred_element_type=F32))
-            hidden = silu_of_half(jnp.dot(hidden, w2h_ref[...], preferred_element_type=F32))
-            output = jnp.dot(hidden, w3_ref[...], preferred_element_type=F32)
-            softplus = jnp.maximum(output, 0.0) + jnp.log(1.0 + jnp.exp(-jnp.abs(output)))
-            output = jnp.where(lane512 < 64, output, softplus * (1.0 / PER_BLOCK)).astype(BF16)
-            prod_ref[c, 2 * half : 2 * half + 2] = output.reshape(2, 128, 128)
-        slot = (1 - dcore) * (x * 2 + core) + dcore * (y * 2 + core)
-
-        @pl.when(k < 7)
+            columns = []
+            for q in (2 * half, 2 * half + 1):
+                _, dcore, dx, dy = ring_device(c, q)
+                for u in range(4):
+                    t = lax.rem((1 - dcore) * place_yz + dcore * place_xz + part * 4 + u, 16)
+                    ri = (1 - dcore) * (t // 2) + dcore * (dy * 2 + t // 8)
+                    rj = (1 - dcore) * (lax.rem(t, 2) * 8 + dx * 2) + dcore * (lax.rem(t, 8) * 2 + 1)
+                    start = pl.multiple_of((ri * 16 + rj) * 128, 128)
+                    columns.append(feat_ref[:, pl.ds(start, 128)])
+            columns = jnp.concatenate(columns, axis=1)
+            hidden = silu_of_half(jnp.dot(w1t_ref[...], columns, preferred_element_type=F32))
+            hidden = silu_of_half(jnp.dot(w2t_ref[...], hidden, preferred_element_type=F32))
+            output = jnp.dot(w3t_ref[...], hidden, preferred_element_type=F32)
+            stress, tangent = output[:64], output[64:]
+            tangent = jnp.maximum(tangent, 0.0) + jnp.log(1.0 + jnp.exp(-jnp.abs(tangent)))
+            output = jnp.concatenate([stress, tangent * (1.0 / PER_BLOCK)], axis=0).astype(BF16)
+            for u in range(8):
+                prod_ref[part * 2 + c, 2 * half + u // 4, u % 4] = output[:, u * 128 : (u + 1) * 128]
+
+        @pl.when(part * 2 + c == 0)
         def _():
-            pltpu.make_async_remote_copy(
-                src_ref=prod_ref.at[c],
-                dst_ref=ring_ref.at[slot, pl.ds(part * 4, 4)],
-                send_sem=ring_send,
-                recv_sem=ring_recv.at[slot],
-                device_id=(dy * 2 + zh, (zl * 4 + dx) * 2 + dcore),
-                device_id_type=MESH,
-            ).start()
-
-        @pl.when(k == 7)
+            pl.semaphore_wait(barrier, len(others))
+            lax.fori_loop(1, 16, send_index, 0)
+
+        for q in range(4):
+            turn, dcore, dx, dy = ring_device(c, q)
+            slot = (1 - dcore) * (x * 2 + core) + dcore * (y * 2 + core)
+
+            def remote():
+                pltpu.make_async_remote_copy(
+                    src_ref=prod_ref.at[part * 2 + c, q],
+                    dst_ref=ring_ref.at[slot, part],
+                    send_sem=ring_send,
+                    recv_sem=ring_recv.at[slot, part],
+                    device_id=(dy * 2 + zh, (zl * 4 + dx) * 2 + dcore),
+                    device_id_type=MESH,
+                ).start()
+
+            if q < 3:
+                remote()
+            else:
+                pl.when(c == 0)(remote)
+
+                @pl.when(c == 1)
+                def _():
+                    ring_ref[slot, part] = prod_ref[part * 2 + c, q]
+
+        return part
+
+    def ring_device(c, q):
+        turn = jnp.where(c == 0, (1, 1, 3, 3)[q], (2, 2, 0, 0)[q])
+        dcore = lax.rem(core + jnp.where(c == 0, (0, 1, 0, 1)[q], (0, 1, 1, 0)[q]), 2)
+        return turn, dcore, lax.rem(x + turn * (1 - dcore), 4), lax.rem(y + turn * dcore, 4)
+
+    mine = pick(x * 2 + core, y * 2 + core)
+
+    def reduce_rows(part):
+        @pl.when(part == 0)
         def _():
-            ring_ref[slot, pl.ds(part * 4, 4)] = prod_ref[c]
+            got = index_ref.at[pl.ds(0, 15)]
+            pltpu.make_async_copy(got, got, index_sem.at[1]).wait()
+
+        for s in range(1, 8):
+            slot = lax.rem(mine + s, 8)
+            got = ring_ref.at[slot, part]
+            pltpu.make_async_copy(got, got, ring_recv.at[slot, part]).wait()
+
+        def one(u, carry):
+            t = lax.rem(place + part * 4 + u, 16)
+            owners = index_ref[t]
+            block = lax.broadcasted_iota(jnp.int32, (256, 128), 0)
+            onehot = jnp.concatenate(
+                [(block == owners[e : e + 1]).astype(F32).astype(BF16) for e in range(8)], axis=1
+            )
+            rows = jnp.concatenate([ring_ref[e, part, u] for e in range(8)], axis=1)
+            plane_out[t] = lax.dot_general(
+                rows, onehot, (((1,), (1,)), ((), ())), preferred_element_type=F32
+            ).astype(BF16)
+
+            @pl.when(part * 4 + u > 0)
+            def _():
+                pltpu.make_async_remote_copy(
+                    src_ref=plane_out.at[t],
+                    dst_ref=plane_ref.at[place],
+                    send_sem=plane_sem.at[0],
+                    recv_sem=plane_sem.at[1],
+                    device_id=plane_device(t),
+                    device_id_type=MESH,
+                ).start()
+
+            @pl.when(part * 4 + u == 0)
+            def _():
+                plane_ref[place] = plane_out[t]
+
+            return carry
+
+        lax.fori_loop(0, 4, one, 0)
+
+    def run_part(part, carry):
+        lax.fori_loop(0, 2, chunk, part)
+
+        @pl.when(part > 0)
+        def _():
+            reduce_rows(part - 1)
 
         return carry
 
-    lax.fori_loop(0, 32, chunk, 0)
-
-    mine = pick(x * 2 + core, y * 2 + core)
-    pltpu.make_async_copy(index_ref.at[pl.ds(0, 15)], index_ref.at[pl.ds(0, 15)], index_sem.at[1]).wait()
-    for s in range(1, 8):
-        slot = lax.rem(mine + s, 8)
-        pltpu.make_async_copy(ring_ref.at[slot], ring_ref.at[slot], ring_recv.at[slot]).wait()
-
-    def reduce_rows(s, carry):
-        t = lax.rem(place + s, 16)
-        owners = index_ref[t]
-        block = lax.broadcasted_iota(jnp.int32, (256, 128), 0)
-        onehot = jnp.concatenate(
-            [(block == owners[e : e + 1]).astype(F32).astype(BF16) for e in range(8)], axis=1
-        )
-        rows = ring_ref[:, t].reshape(1024, 128)
-        plane_out[t] = jnp.dot(onehot, rows, preferred_element_type=F32).astype(BF16)
-
-        @pl.when(s < 16)
-        def _():
-            pltpu.make_async_remote_copy(
-                src_ref=plane_out.at[t],
-                dst_ref=plane_ref.at[place],
-                send_sem=plane_sem.at[0],
-                recv_sem=plane_sem.at[1],
-                device_id=plane_device(t),
-                device_id_type=MESH,
-            ).start()
-
-        @pl.when(s == 16)
-        def _():
-            plane_ref[place] = plane_out[t]
-
-        return carry
-
-    lax.fori_loop(1, 17, reduce_rows, 0)
+    lax.fori_loop(0, 4, run_part, 0)
+    reduce_rows(jnp.int32(3))
     for load in loads[1:]:
         load.wait()
     jac_ref, diag_ref, u_ref, w_ref, d_ref, s_ref, q_ref, zz_ref = (vectors.at[k] for k in range(8))
@@ -249,7 +281,7 @@
     total = plane_ref[0].astype(F32)
     for t in range(1, 16):
         total = total + plane_ref[t].astype(F32)
-    fields = total.T
+    fields = total
     residual_ref[EVEN, :] = fields[:64, :128]
     residual_ref[ODD, :] = fields[:64, 128:]
     diag_ref[EVEN, :] = fields[64:, :128] + DIAG_SHIFT
@@ -434,9 +466,15 @@
         for stage, (buffer, count) in enumerate([(sum_a, 7), (sum_b, 15)]):
             mover = buffer.at[it, pl.ds(0, count)]
             pltpu.make_async_copy(mover, mover, sum_send.at[it, stage]).wait()
-    pltpu.make_async_copy(prod_ref.at[pl.ds(0, 28)], prod_ref.at[pl.ds(0, 28)], ring_send).wait()
+    out = prod_ref.at[pl.ds(0, 7)]
+    pltpu.make_async_copy(out, out, ring_send).wait()
     pltpu.make_async_copy(plane_ref.at[pl.ds(0, 15)], plane_ref.at[pl.ds(0, 15)], plane_sem.at[0]).wait()
     pltpu.make_async_copy(index_ref.at[pl.ds(0, 15)], index_ref.at[pl.ds(0, 15)], index_sem.at[0]).wait()
+
+
+def hand_over(adjoint_ref, residual_ref, adjoint_out, residual_out):
+    adjoint_out[...] = adjoint_ref[...]
+    residual_out[...] = residual_ref[...]
 
 
 def local(*args):
@@ -454,12 +492,12 @@
         x_map,
         y_map,
     ) = args
-    features = quad_features.reshape(16384, FEATURES)
+    features = quad_features.reshape(16384, FEATURES).T
     tiles = [t.reshape(64, 128, 128) for t in (diag_tiles, x_tiles, y_tiles, p_tiles)]
     owners = quad_block.reshape(128, 128)
-    cols = jnp.broadcast_to(tile_cols.reshape(1, 256), (8, 256))
-    xmap = jnp.broadcast_to(x_map.reshape(1, 128), (8, 128))
-    yswap = jnp.broadcast_to(y_map[0, 0, 0], (8, 128))
+    cols = tile_cols.reshape(1, 256)
+    xmap = x_map.reshape(1, 128)
+    yswap = y_map.reshape(1, 2)
     hbm = pl.BlockSpec(memory_space=pl.ANY)
     vmem = pl.BlockSpec(memory_space=pltpu.VMEM)
     square = pltpu.VMEM((128, 128), F32)
@@ -473,13 +511,14 @@
         in_specs=[hbm, vmem, vmem, vmem, vmem, hbm, hbm, hbm, hbm, vmem, vmem, vmem],
         out_specs=[vmem, vmem],
         scratch_shapes=[
-            pltpu.VMEM((16384, FEATURES), BF16),
-            pltpu.VMEM((64, 512), BF16),
+            pltpu.VMEM((FEATURES, 16384), BF16),
+            pltpu.VMEM((512, 64), BF16),
             pltpu.VMEM((512, 512), BF16),
-            pltpu.VMEM((32, 4, 128, 128), BF16),
-            pltpu.VMEM((8, 16, 128, 128), BF16),
-            pltpu.VMEM((16, 256, 128), BF16),
-            pltpu.VMEM((16, 256, 128), BF16),
+            pltpu.VMEM((128, 512), BF16),
+            pltpu.VMEM((8, 4, 4, 128, 128), BF16),
+            pltpu.VMEM((8, 4, 4, 128, 128), BF16),
+            pltpu.VMEM((16, 128, 256), BF16),
+            pltpu.VMEM((16, 128, 256), BF16),
             pltpu.VMEM((16, 8, 128), jnp.int32),
             pltpu.VMEM((16, 8, 128), jnp.int32),
             tile,
@@ -505,7 +544,7 @@
             pltpu.VMEM((ITERS, 16, 2, 128), F32),
             dma((5,)),
             dma,
-            dma((8,)),
+            dma((8, 4)),
             dma((2,)),
             dma((2,)),
             dma((4 * ITERS,)),
@@ -517,6 +556,12 @@
             collective_id=0, has_side_effects=True, vmem_limit_bytes=56 * 2**20
         ),
     )(features, w_first, w_second, w_third, owners, *tiles, cols, xmap, yswap)
+    adjoint, residual = pl.pallas_call(
+        hand_over,
+        out_shape=[jax.ShapeDtypeStruct((128, 128), F32)] * 2,
+        in_specs=[vmem, vmem],
+        out_specs=[vmem, vmem],
+    )(adjoint, residual)
     return adjoint.reshape(64, 2, 128), residual.reshape(64, 2, 128)
 
 

time: 104 us -> 81.1 us (0.78)
  local copies, waits for them, and re-layouts: 11.5 us -> 0 us
  Pallas kernels: 91.7 us -> 80.3 us
    pallas_call x1, Pallas kernels: 91.7 us -> 78.8 us  [local(): pl.pallas_call(kernel, out_shape=[jax.ShapeDtypeStruct((128, 128), F32)]...]
    unnamed x3 -> x0, local copies, waits for them, and re-layouts: 7.73 us -> none
    broadcast_in_dim x3 -> x0, local copies, waits for them, and re-layouts: 3.76 us -> none  [the longest x1 1.28 us: local(): cols = jnp.broadcast_to(tile_cols.reshape(1, 256), (8, 256))]
    pallas_call x0 -> x1, Pallas kernels: none -> 1.53 us  [local(): pl.pallas_call(hand_over, out_shape=[jax.ShapeDtypeStruct((128, 128), F32...]
where the time goes in v3:
time: 81.1 us; the launch traced here: 80.9 us
  Pallas kernels  80.3 us (99%)
    pallas_call x1, Pallas kernels, local(): pl.pallas_call(kernel, out_shape=[jax.ShapeDtypeStruct((128, 128), F32)]...  78.8 us

profile of v3, /device:TPU:1, one launch (start us, length us, event | category | flops | bytes accessed | tf_op | source)
XLA Modules:
  0.0 80.9 jit_solution(17662492923529924808)
XLA Ops:
  0.6 78.8 %shard_map.131 = (f32[128,128]{1,0:T(8,128)}, f32[128,128]{1,0:T(8,128)}) custom-call(bf16[64,16384]{1,0:T(8,128)(2,1)} %bitcast.17, bf16[64,512]{1,0:T(8,128)(2,1)} %w1_ref.1, bf16[512,512]{1,0:T(8,128)(2,1)} %w2_ref.1, bf16[512,128]{1,0:T(8,128)(2,1)} %w3_ref.1, s32[128,128]{1,0:T(8,128)} %bitcast.18, f32[64,128,128]{2,1,0:T(8,128)} %bitcast.13, ...), custom_call_target="tpu_custom_call" | custom-call | tf_op jit(solution)/shard_map/pallas_call | solution.py:508
  79.4 1.5 %shard_map.132 = (f32[128,128]{1,0:T(8,128)}, f32[128,128]{1,0:T(8,128)}) custom-call(f32[128,128]{1,0:T(8,128)} %get-tuple-element.6.adjoint_ref, f32[128,128]{1,0:T(8,128)} %get-tuple-element.7.residual_ref), custom_call_target="tpu_custom_call" | custom-call | tf_op jit(solution)/shard_map/pallas_call | solution.py:559

commit v4 on v3

--- a/solution.py
+++ b/solution.py
@@ -161,13 +161,18 @@
 
     loads[0].wait()
 
-    def chunk(c, part):
+    def ring_device(q):
+        turn = (1, 1, 3, 3, 2, 2, 0, 0)[q]
+        dcore = (core, 1 - core, core, 1 - core, core, 1 - core, 1 - core, core)[q]
+        return dcore, lax.rem(x + turn * (1 - dcore), 4), lax.rem(y + turn * dcore, 4)
+
+    def network(part):
         for half in range(2):
             columns = []
-            for q in (2 * half, 2 * half + 1):
-                _, dcore, dx, dy = ring_device(c, q)
-                for u in range(4):
-                    t = lax.rem((1 - dcore) * place_yz + dcore * place_xz + part * 4 + u, 16)
+            for q in range(4 * half, 4 * half + 4):
+                dcore, dx, dy = ring_device(q)
+                for u in range(2):
+                    t = lax.rem((1 - dcore) * place_yz + dcore * place_xz + part * 2 + u, 16)
                     ri = (1 - dcore) * (t // 2) + dcore * (dy * 2 + t // 8)
                     rj = (1 - dcore) * (lax.rem(t, 2) * 8 + dx * 2) + dcore * (lax.rem(t, 8) * 2 + 1)
                     start = pl.multiple_of((ri * 16 + rj) * 128, 128)
@@ -180,20 +185,21 @@
             tangent = jnp.maximum(tangent, 0.0) + jnp.log(1.0 + jnp.exp(-jnp.abs(tangent)))
             output = jnp.concatenate([stress, tangent * (1.0 / PER_BLOCK)], axis=0).astype(BF16)
             for u in range(8):
-                prod_ref[part * 2 + c, 2 * half + u // 4, u % 4] = output[:, u * 128 : (u + 1) * 128]
-
-        @pl.when(part * 2 + c == 0)
+                prod_ref[part, 4 * half + u // 2, u % 2] = output[:, u * 128 : (u + 1) * 128]
+
+        @pl.when(part == 0)
         def _():
             pl.semaphore_wait(barrier, len(others))
             lax.fori_loop(1, 16, send_index, 0)
 
-        for q in range(4):
-            turn, dcore, dx, dy = ring_device(c, q)
+        for q in range(8):
+            dcore, dx, dy = ring_device(q)
             slot = (1 - dcore) * (x * 2 + core) + dcore * (y * 2 + core)
-
-            def remote():
+            if q == 7:
+                ring_ref[slot, part] = prod_ref[part, q]
+            else:
                 pltpu.make_async_remote_copy(
-                    src_ref=prod_ref.at[part * 2 + c, q],
+                    src_ref=prod_ref.at[part, q],
                     dst_ref=ring_ref.at[slot, part],
                     send_sem=ring_send,
                     recv_sem=ring_recv.at[slot, part],
@@ -201,22 +207,6 @@
                     device_id_type=MESH,
                 ).start()
 
-            if q < 3:
-                remote()
-            else:
-                pl.when(c == 0)(remote)
-
-                @pl.when(c == 1)
-                def _():
-                    ring_ref[slot, part] = prod_ref[part * 2 + c, q]
-
-        return part
-
-    def ring_device(c, q):
-        turn = jnp.where(c == 0, (1, 1, 3, 3)[q], (2, 2, 0, 0)[q])
-        dcore = lax.rem(core + jnp.where(c == 0, (0, 1, 0, 1)[q], (0, 1, 1, 0)[q]), 2)
-        return turn, dcore, lax.rem(x + turn * (1 - dcore), 4), lax.rem(y + turn * dcore, 4)
-
     mine = pick(x * 2 + core, y * 2 + core)
 
     def reduce_rows(part):
@@ -229,9 +219,8 @@
             slot = lax.rem(mine + s, 8)
             got = ring_ref.at[slot, part]
             pltpu.make_async_copy(got, got, ring_recv.at[slot, part]).wait()
-
-        def one(u, carry):
-            t = lax.rem(place + part * 4 + u, 16)
+        for u in range(2):
+            t = lax.rem(place + part * 2 + u, 16)
             owners = index_ref[t]
             block = lax.broadcasted_iota(jnp.int32, (256, 128), 0)
             onehot = jnp.concatenate(
@@ -242,39 +231,43 @@
                 rows, onehot, (((1,), (1,)), ((), ())), preferred_element_type=F32
             ).astype(BF16)
 
-            @pl.when(part * 4 + u > 0)
-            def _():
-                pltpu.make_async_remote_copy(
-                    src_ref=plane_out.at[t],
-                    dst_ref=plane_ref.at[place],
-                    send_sem=plane_sem.at[0],
-                    recv_sem=plane_sem.at[1],
-                    device_id=plane_device(t),
-                    device_id_type=MESH,
-                ).start()
-
-            @pl.when(part * 4 + u == 0)
-            def _():
-                plane_ref[place] = plane_out[t]
-
-            return carry
-
-        lax.fori_loop(0, 4, one, 0)
+        def remote(u):
+            t = lax.rem(place + part * 2 + u, 16)
+            pltpu.make_async_remote_copy(
+                src_ref=plane_out.at[t],
+                dst_ref=plane_ref.at[place],
+                send_sem=plane_sem.at[0],
+                recv_sem=plane_sem.at[1],
+                device_id=plane_device(t),
+                device_id_type=MESH,
+            ).start()
+
+        pl.when(part > 0)(functools.partial(remote, 0))
+        remote(1)
+
+        @pl.when(part == 0)
+        def _():
+            plane_ref[place] = plane_out[place]
 
     def run_part(part, carry):
-        lax.fori_loop(0, 2, chunk, part)
-
-        @pl.when(part > 0)
+        network(part)
+
+        @pl.when(part > 1)
         def _():
-            reduce_rows(part - 1)
+            reduce_rows(part - 2)
 
         return carry
 
-    lax.fori_loop(0, 4, run_part, 0)
-    reduce_rows(jnp.int32(3))
+    lax.fori_loop(0, 8, run_part, 0)
+
+    def run_rest(part, carry):
+        reduce_rows(part)
+        return carry
+
+    lax.fori_loop(6, 8, run_rest, 0)
     for load in loads[1:]:
         load.wait()
-    jac_ref, diag_ref, u_ref, w_ref, d_ref, s_ref, q_ref, zz_ref = (vectors.at[k] for k in range(8))
+    jac_ref, off_ref, sum_ref, *krylov = (vectors.at[k] for k in range(8))
     for k in range(64):
         jac_ref[2 * k : 2 * k + 2, :] = e_ref[k, 2 * k : 2 * k + 2, :]
     pltpu.make_async_copy(plane_ref.at[pl.ds(0, 15)], plane_ref.at[pl.ds(0, 15)], plane_sem.at[1]).wait()
@@ -284,9 +277,10 @@
     fields = total
     residual_ref[EVEN, :] = fields[:64, :128]
     residual_ref[ODD, :] = fields[:64, 128:]
-    diag_ref[EVEN, :] = fields[64:, :128] + DIAG_SHIFT
-    diag_ref[ODD, :] = fields[64:, 128:] + DIAG_SHIFT
-    jac_ref[...] = diag_ref[...] + 2.0 * jac_ref[...]
+    off_ref[...] = -2.0 * jac_ref[...]
+    jac_ref[EVEN, :] = fields[64:, :128] + DIAG_SHIFT
+    jac_ref[ODD, :] = fields[64:, 128:] + DIAG_SHIFT
+    jac_ref[...] = jac_ref[...] - off_ref[...]
 
     x_next, x_prev = (lax.rem(i + 1, 8), j), (lax.rem(i + 7, 8), j)
     y_next, y_prev = (i, lax.rem(j + 1, 16)), (i, lax.rem(j + 15, 16))
@@ -344,42 +338,61 @@
 
     index_b = i * 2 + zl
 
-    def sum_begin(it, first, second):
-        sum_a[it, jl] = jnp.concatenate(
-            [jnp.sum(first, axis=0, keepdims=True), jnp.sum(second, axis=0, keepdims=True)], axis=0
+    def sum_begin(rows):
+        sum_a[jl] = jnp.concatenate(
+            [jnp.sum(row, axis=0, keepdims=True) for row in rows] + [jnp.zeros((8 - len(rows), 128), F32)], axis=0
         )
         for k in range(1, 8):
             pltpu.make_async_remote_copy(
-                src_ref=sum_a.at[it, jl],
-                dst_ref=sum_a.at[it, jl],
-                send_sem=sum_send.at[it, 0],
-                recv_sem=sum_recv.at[it, 0],
+                src_ref=sum_a.at[jl],
+                dst_ref=sum_a.at[jl],
+                send_sem=sum_send.at[0],
+                recv_sem=sum_recv.at[0],
                 device_id=(i, zl * 8 + lax.rem(jl + k, 8)),
                 device_id_type=MESH,
             ).start()
 
-    def sum_middle(it):
-        pltpu.make_async_copy(sum_a.at[it, pl.ds(0, 7)], sum_a.at[it, pl.ds(0, 7)], sum_recv.at[it, 0]).wait()
-        sum_b[it, index_b] = jnp.sum(sum_a[it], axis=0)
+    def sum_middle():
+        pltpu.make_async_copy(sum_a.at[pl.ds(0, 7)], sum_a.at[pl.ds(0, 7)], sum_recv.at[0]).wait()
+        sum_b[index_b] = jnp.sum(sum_a[...], axis=0)
         for k in range(1, 16):
             peer = lax.rem(index_b + k, 16)
             pltpu.make_async_remote_copy(
-                src_ref=sum_b.at[it, index_b],
-                dst_ref=sum_b.at[it, index_b],
-                send_sem=sum_send.at[it, 1],
-                recv_sem=sum_recv.at[it, 1],
+                src_ref=sum_b.at[index_b],
+                dst_ref=sum_b.at[index_b],
+                send_sem=sum_send.at[1],
+                recv_sem=sum_recv.at[1],
                 device_id=(peer // 2, lax.rem(peer, 2) * 8 + jl),
                 device_id_type=MESH,
             ).start()
 
-    def sum_end(it):
-        pltpu.make_async_copy(sum_b.at[it, pl.ds(0, 15)], sum_b.at[it, pl.ds(0, 15)], sum_recv.at[it, 1]).wait()
-        total = jnp.sum(jnp.sum(sum_b[it], axis=0), axis=1, keepdims=True)
-        return total[0:1], total[1:2]
+    def sum_end():
+        pltpu.make_async_copy(sum_b.at[pl.ds(0, 15)], sum_b.at[pl.ds(0, 15)], sum_recv.at[1]).wait()
+        total = jnp.sum(jnp.sum(sum_b[...], axis=0), axis=1, keepdims=True)
+        return [total[k : k + 1] for k in range(2 * ITERS)]
 
     sent = []
 
-    def apply(it, z, between):
+    def gather_p(even, odd, transposed):
+        flat = permute(jnp.concatenate([even, odd], axis=1), mp_ref[...], transposed)
+        return flat[:, :128], flat[:, 128:]
+
+    def out_x(it):
+        tmp_ref[...] = transposed_pass(x_ref)
+        ix_out[it] = permute(tmp_ref[ODD, :], mx_ref[...], True)
+        sent.append(send(ix_out.at[it], ix_in.at[it], 4 * it + 2, x_next))
+        acc_ref[ODD, :] += tmp_ref[EVEN, :]
+        return sent[-1]
+
+    def out_y(it):
+        turned = transposed_pass(y_ref)
+        iy_out[it] = swap_pairs(turned.T[120:128], yswap)
+        sent.append(send(iy_out.at[it], iy_in.at[it], 4 * it + 3, y_next))
+        acc_ref[...] += jnp.where(lane == 0, 0.0, pltpu.roll(turned, 1, 1))
+        return sent[-1]
+
+    def couple(it, z, moments):
+        last = it + 1 == ITERS
         tmp_ref[...] = z
         z_even, z_odd = tmp_ref[EVEN, :], tmp_ref[ODD, :]
         hx_out[it] = z_even
@@ -389,23 +402,15 @@
         for q in range(4):
             vb_ref[:, 2 * q, :] = z_even
             vb_ref[:, 2 * q + 1, :] = z_odd
-        tmp_ref[...] = transposed_pass(x_ref)
-        ix_out[it] = permute(tmp_ref[ODD, :], mx_ref[...], True)
-        ix = send(ix_out.at[it], ix_in.at[it], 4 * it + 2, x_next)
-        turned = transposed_pass(y_ref)
-        iy_out[it] = swap_pairs(turned.T[120:128], yswap)
-        iy = send(iy_out.at[it], iy_in.at[it], 4 * it + 3, y_next)
-        acc_ref[...] = diag_ref[...] * z + jnp.where(lane == 0, 0.0, pltpu.roll(turned, 1, 1))
-        acc_ref[ODD, :] += tmp_ref[EVEN, :]
-        between()
+        acc_ref[...] = off_ref[...] * z
+        if not last:
+            ix, iy = out_x(it), out_y(it)
         acc_ref[...] += both_pass(e_ref, z, True)
-        flat = permute(jnp.concatenate([z_even, z_odd], axis=1), mp_ref[...], False)
-        tmp_ref[EVEN, :] = flat[:, :128]
-        tmp_ref[ODD, :] = flat[:, 128:]
+        tmp_ref[EVEN, :], tmp_ref[ODD, :] = gather_p(z_even, z_odd, False)
         tmp_ref[...] = both_pass(p_ref, tmp_ref[...], False)
-        flat = permute(jnp.concatenate([tmp_ref[EVEN, :], tmp_ref[ODD, :]], axis=1), mp_ref[...], True)
-        acc_ref[EVEN, :] += flat[:, :128]
-        acc_ref[ODD, :] += flat[:, 128:]
+        add_even, add_odd = gather_p(tmp_ref[EVEN, :], tmp_ref[ODD, :], True)
+        acc_ref[EVEN, :] += add_even
+        acc_ref[ODD, :] += add_odd
         hx.wait_recv()
         tmp_ref[EVEN, :] = z_odd
         tmp_ref[ODD, :] = permute(hx_in[it], mx_ref[...], False) * edge_x
@@ -417,55 +422,57 @@
             total = red_ref[:, a, :]
             for q in range(1, 4):
                 total = total + red_ref[:, 2 * q + a, :]
-            acc_ref[part, :] += total
+            sum_ref[part, :] = total
+        acc_ref[...] += sum_ref[...]
+        if last:
+            sum_begin(moments + [z * (off_ref[...] * z + 2.0 * sum_ref[...])])
+            ix, iy = out_x(it), out_y(it)
+            sum_middle()
         ix.wait_recv()
         acc_ref[EVEN, :] += ix_in[it] * start_x
         iy.wait_recv()
         acc_ref[...] += jnp.where(lane == 0, column(iy_in[it, 7:8]) * start_y, 0.0)
-        sent.extend([hx, hy, ix, iy])
+        sent.extend([hx, hy])
         return acc_ref[...]
 
-    u_ref[...] = residual_ref[...] / jac_ref[...]
-    w_ref[...] = apply(0, u_ref[...], lambda: None)
-    alpha = gamma_old = None
+    v_refs, r_refs = krylov[:ITERS], [residual_ref] + krylov[ITERS:]
+    moments = []
     for it in range(ITERS):
-        last = it + 1 == ITERS
-        sum_begin(it, residual_ref[...] * u_ref[...], w_ref[...] * u_ref[...])
-        if last:
-            sum_middle(it)
-        else:
-            m = w_ref[...] / jac_ref[...]
-            n = apply(it + 1, m, functools.partial(sum_middle, it))
-        gamma, delta = sum_end(it)
-        if it == 0:
-            alpha = gamma / delta
-            direction, image = u_ref[...], w_ref[...]
-            adjoint_ref[...] = alpha * direction
-        else:
-            beta = gamma / gamma_old
-            alpha = gamma / (delta - beta * gamma / alpha)
-            direction = u_ref[...] + beta * d_ref[...]
-            image = w_ref[...] + beta * s_ref[...]
-            adjoint_ref[...] += alpha * direction
-            if not last:
-                m = m + beta * q_ref[...]
-                n = n + beta * zz_ref[...]
-        gamma_old = gamma
-        residual_ref[...] -= alpha * image
-        if not last:
-            d_ref[...] = direction
-            s_ref[...] = image
-            q_ref[...] = m
-            zz_ref[...] = n
-            u_ref[...] -= alpha * m
-            w_ref[...] -= alpha * n
+        v_refs[it][...] = r_refs[it][...] / jac_ref[...]
+        moments.append(r_refs[it][...] * v_refs[it][...])
+        image = couple(it, v_refs[it][...], moments)
+        if it + 1 < ITERS:
+            r_refs[it + 1][...] = image
+            moments.append(image * v_refs[it][...])
+    nu = sum_end()
+
+    def ratio(above, below):
+        return jnp.where(below == 0.0, 0.0, above / jnp.where(below == 0.0, 1.0, below))
+
+    def form(first, second):
+        return sum(a * b * nu[k + m] for k, a in enumerate(first) for m, b in enumerate(second))
+
+    one = jnp.ones((1, 1), F32)
+    res, direction, solved = [one], [one], [0.0] * ITERS
+    gamma = nu[0]
+    for it in range(ITERS):
+        moved = [a + b for a, b in zip(direction + [0.0 * one], [0.0 * one] + direction)]
+        alpha = ratio(gamma, form(direction, moved))
+        solved = [a + alpha * b for a, b in zip(solved, direction)] + solved[len(direction) :]
+        res = [a - alpha * b for a, b in zip(res + [0.0 * one], moved)]
+        if it + 1 < ITERS:
+            gamma_next = form(res, res)
+            beta = ratio(gamma_next, gamma)
+            direction = [a + beta * b for a, b in zip(res, direction + [0.0 * one])]
+            gamma = gamma_next
+    adjoint_ref[...] = sum(a * v[...] for a, v in zip(solved, v_refs))
+    residual_ref[...] = sum(a * r[...] for a, r in zip(res, r_refs)) + res[ITERS] * image
 
     for copy in sent:
         copy.wait_send()
-    for it in range(ITERS):
-        for stage, (buffer, count) in enumerate([(sum_a, 7), (sum_b, 15)]):
-            mover = buffer.at[it, pl.ds(0, count)]
-            pltpu.make_async_copy(mover, mover, sum_send.at[it, stage]).wait()
+    for stage, (buffer, count) in enumerate([(sum_a, 7), (sum_b, 15)]):
+        mover = buffer.at[pl.ds(0, count)]
+        pltpu.make_async_copy(mover, mover, sum_send.at[stage]).wait()
     out = prod_ref.at[pl.ds(0, 7)]
     pltpu.make_async_copy(out, out, ring_send).wait()
     pltpu.make_async_copy(plane_ref.at[pl.ds(0, 15)], plane_ref.at[pl.ds(0, 15)], plane_sem.at[0]).wait()
@@ -515,8 +522,8 @@
             pltpu.VMEM((512, 64), BF16),
             pltpu.VMEM((512, 512), BF16),
             pltpu.VMEM((128, 512), BF16),
-            pltpu.VMEM((8, 4, 4, 128, 128), BF16),
-            pltpu.VMEM((8, 4, 4, 128, 128), BF16),
+            pltpu.VMEM((8, 8, 2, 128, 128), BF16),
+            pltpu.VMEM((8, 8, 2, 128, 128), BF16),
             pltpu.VMEM((16, 128, 256), BF16),
             pltpu.VMEM((16, 128, 256), BF16),
             pltpu.VMEM((16, 8, 128), jnp.int32),
@@ -540,17 +547,17 @@
             strip,
             halves,
             strip,
-            pltpu.VMEM((ITERS, 8, 2, 128), F32),
-            pltpu.VMEM((ITERS, 16, 2, 128), F32),
+            pltpu.VMEM((8, 8, 128), F32),
+            pltpu.VMEM((16, 8, 128), F32),
             dma((5,)),
             dma,
-            dma((8, 4)),
+            dma((8, 8)),
             dma((2,)),
             dma((2,)),
             dma((4 * ITERS,)),
             dma((4 * ITERS,)),
-            dma((ITERS, 2)),
-            dma((ITERS, 2)),
+            dma((2,)),
+            dma((2,)),
         ],
         compiler_params=pltpu.CompilerParams(
             collective_id=0, has_side_effects=True, vmem_limit_bytes=56 * 2**20

time: 81.1 us -> 76.4 us (0.942)
  Pallas kernels: 80.3 us -> 75.6 us
    pallas_call x1, Pallas kernels: 78.8 us -> 74.1 us  [local(): pl.pallas_call(kernel, out_shape=[jax.ShapeDtypeStruct((128, 128), F32)]...]
where the time goes in v4:
time: 76.4 us; the launch traced here: 76.2 us
  Pallas kernels  75.6 us (99%)
    pallas_call x1, Pallas kernels, local(): pl.pallas_call(kernel, out_shape=[jax.ShapeDtypeStruct((128, 128), F32)]...  74.1 us
    pallas_call x1, Pallas kernels, local(): pl.pallas_call(hand_over, out_shape=[jax.ShapeDtypeStruct((128, 128), F32...  1.53 us

profile of v4, /device:TPU:1, one launch (start us, length us, event | category | flops | bytes accessed | tf_op | source)
XLA Modules:
  0.0 76.2 jit_solution(15443238794533737500)
XLA Ops:
  0.6 74.1 %shard_map.131 = (f32[128,128]{1,0:T(8,128)}, f32[128,128]{1,0:T(8,128)}) custom-call(bf16[64,16384]{1,0:T(8,128)(2,1)} %bitcast.17, bf16[64,512]{1,0:T(8,128)(2,1)} %w1_ref.1, bf16[512,512]{1,0:T(8,128)(2,1)} %w2_ref.1, bf16[512,128]{1,0:T(8,128)(2,1)} %w3_ref.1, s32[128,128]{1,0:T(8,128)} %bitcast.18, f32[64,128,128]{2,1,0:T(8,128)} %bitcast.13, ...), custom_call_target="tpu_custom_call" | custom-call | tf_op jit(solution)/shard_map/pallas_call | solution.py:515
  74.7 1.5 %shard_map.132 = (f32[128,128]{1,0:T(8,128)}, f32[128,128]{1,0:T(8,128)}) custom-call(f32[128,128]{1,0:T(8,128)} %get-tuple-element.6.adjoint_ref, f32[128,128]{1,0:T(8,128)} %get-tuple-element.7.residual_ref), custom_call_target="tpu_custom_call" | custom-call | tf_op jit(solution)/shard_map/pallas_call | solution.py:566

commit v5 on v4

--- a/solution.py
+++ b/solution.py
@@ -9,6 +9,7 @@
 
 FEATURES = 64
 ITERS = 3
+UNROLL = 8
 PER_BLOCK = 64
 DIAG_SHIFT = 5.0
 MESH = pl.DeviceIdType.MESH
@@ -105,6 +106,7 @@
     y, zh = i // 2, lax.rem(i, 2)
     zl, jl = j // 8, lax.rem(j, 8)
     x, core = jl // 2, lax.rem(j, 2)
+    z = zh * 2 + zl
 
     loads = [
         pltpu.make_async_copy(src, dst, local_sem.at[k])
@@ -118,42 +120,67 @@
     def pick(first, second):
         return first * (1 - core) + second * core
 
-    others = [(i, lax.rem(j + k, 16)) for k in range(1, 16)]
-    others += [(lax.rem(i + k, 8), j) for k in range(1, 8)]
-    others += [(lax.rem(i + k, 8), lax.rem(j + 8, 16)) for k in range(1, 8)]
-    others += [(lax.rem(y + k, 4) * 2 + zh, j + 1 - 2 * core) for k in range(1, 4)]
-    others += [(y * 2 + 1 - zh, lax.rem(j + 2 * k, 16)) for k in range(1, 8)]
     barrier = pltpu.get_barrier_semaphore()
-    for other in others:
+
+    def greet(k, carry):
+        other = (lax.rem(i + k // 16, 8), lax.rem(j + lax.rem(k, 16), 16))
         pl.semaphore_signal(barrier, inc=1, device_id=other, device_id_type=MESH)
+        return carry
+
+    lax.fori_loop(1, 128, greet, 0)
 
     w1t_ref[...] = (w1_ref[...].astype(F32) * 0.5).T.astype(BF16)
     w2t_ref[...] = (w2_ref[...].astype(F32) * 0.5).T.astype(BF16)
     w3t_ref[...] = w3_ref[...].astype(F32).T.astype(BF16)
 
-    place_yz, place_xz = i * 2 + zl, zh * 8 + zl * 4 + x
-    place = pick(place_yz, place_xz)
-
-    def plane_device(t):
-        return pick(t // 2, y * 2 + t // 8), pick(lax.rem(t, 2) * 8 + x * 2, lax.rem(t, 8) * 2 + 1)
-
-    for t in range(16):
+    kind = lax.rem(x + y + z, 4)
+    flat = jnp.where(kind == 0, 1, 0)
+
+    def mod4(value):
+        return lax.rem(value + 16, 4)
+
+    def device(dx, dy, dz, dcore):
+        return dy * 2 + dz // 2, (lax.rem(dz, 2) * 4 + dx) * 2 + dcore
+
+    def receiver(dx, dy, dz, dcore, part, u):
+        if u == 0:
+            ry = mod4(dy + part)
+            return mod4(-ry - dz), ry, dz
+        along = dcore * dx + (1 - dcore) * dy
+        moved = mod4(along + part)
+        kept = dcore * dy + (1 - dcore) * dx
+        return dcore * moved + (1 - dcore) * kept, dcore * kept + (1 - dcore) * moved, mod4(u - moved - kept)
+
+    def summer(s):
+        a, b = s // 4, s % 4
+        sx, sy, sz = mod4(x + (flat + (1 - flat) * core) * a), 0, 0
+        sy = mod4(y + flat * b + (1 - flat) * (1 - core) * a)
+        sz = mod4(z + (1 - flat) * b)
+        return sx, sy, sz
+
+    def index_place(s):
+        return flat * ((4 - s % 4) % 4) * 4 + (1 - flat) * (((4 - s // 4) % 4) * 4 + kind)
+
+    for s in range(16):
+        sx, sy, sz = summer(s)
         for q in range(4):
-            first = pick((t // 2) * 16 + (t % 2) * 8 + q * 2, (q * 2 + t // 8) * 16 + (t % 8) * 2)
-            index_out[t, 2 * q : 2 * q + 2, :] = owner_ref[pl.ds(first, 2), :]
-    index_ref[place] = index_out[place]
-
-    def send_index(s, carry):
-        t = lax.rem(place + s, 16)
-        pltpu.make_async_remote_copy(
-            src_ref=index_out.at[t],
-            dst_ref=index_ref.at[place],
-            send_sem=index_sem.at[0],
-            recv_sem=index_sem.at[1],
-            device_id=plane_device(t),
-            device_id_type=MESH,
-        ).start()
-        return carry
+            ex = flat * sx + (1 - flat) * pick(q, sx)
+            ey = flat * sy + (1 - flat) * pick(sy, q)
+            ez = flat * q + (1 - flat) * sz
+            ei, ej = device(ex, ey, ez, 0)
+            index_out[s, 2 * q : 2 * q + 2, :] = owner_ref[pl.ds(ei * 16 + ej, 2), :]
+    index_ref[index_place(0)] = index_out[0]
+
+    def send_indices():
+        for s in range(1, 16):
+            pltpu.make_async_remote_copy(
+                src_ref=index_out.at[s],
+                dst_ref=index_ref.at[index_place(s)],
+                send_sem=index_sem.at[0],
+                recv_sem=index_sem.at[1],
+                device_id=device(*summer(s), core),
+                device_id_type=MESH,
+            ).start()
 
     mp_ref[...] = (lax.broadcasted_iota(jnp.int32, (256, 256), 0) == cols_ref[0:1]).astype(F32).astype(BF16)
     mx_ref[...] = (lax.broadcasted_iota(jnp.int32, (128, 128), 0) == xmap_ref[0:1]).astype(F32).astype(BF16)
@@ -161,23 +188,27 @@
 
     loads[0].wait()
 
-    def ring_device(q):
-        turn = (1, 1, 3, 3, 2, 2, 0, 0)[q]
-        dcore = (core, 1 - core, core, 1 - core, core, 1 - core, 1 - core, core)[q]
-        return dcore, lax.rem(x + turn * (1 - dcore), 4), lax.rem(y + turn * dcore, 4)
-
-    def network(part):
+    def routes(h):
+        found = []
+        for turn in ((1, 3), (2, 0))[h]:
+            for own in (0, 1) if turn else (1, 0):
+                dcore = own * (1 - core) + (1 - own) * core
+                at = (mod4(x + turn * (1 - dcore)), mod4(y + turn * dcore), z, dcore)
+                found.append((False, at, ((1 - dcore) * x + dcore * y) * 2 + core))
+        for turn in ((1, 3), (2, 0))[h]:
+            for own in (0, 1) if turn else (1, 0):
+                dcore = own * (1 - core) + (1 - own) * core
+                found.append((True, (x, y, mod4(z + turn), dcore), z * 2 + core))
+        return found
+
+    def network(part, h):
+        blocks = []
+        for along_z, at, _ in routes(h):
+            for u in (0,) if along_z else (1, 2, 3):
+                ri, rj = device(*receiver(*at, part, u), at[3])
+                blocks.append(pl.multiple_of((ri * 16 + rj) * 128, 128))
         for half in range(2):
-            columns = []
-            for q in range(4 * half, 4 * half + 4):
-                dcore, dx, dy = ring_device(q)
-                for u in range(2):
-                    t = lax.rem((1 - dcore) * place_yz + dcore * place_xz + part * 2 + u, 16)
-                    ri = (1 - dcore) * (t // 2) + dcore * (dy * 2 + t // 8)
-                    rj = (1 - dcore) * (lax.rem(t, 2) * 8 + dx * 2) + dcore * (lax.rem(t, 8) * 2 + 1)
-                    start = pl.multiple_of((ri * 16 + rj) * 128, 128)
-                    columns.append(feat_ref[:, pl.ds(start, 128)])
-            columns = jnp.concatenate(columns, axis=1)
+            columns = jnp.concatenate([feat_ref[:, pl.ds(b, 128)] for b in blocks[8 * half : 8 * half + 8]], axis=1)
             hidden = silu_of_half(jnp.dot(w1t_ref[...], columns, preferred_element_type=F32))
             hidden = silu_of_half(jnp.dot(w2t_ref[...], hidden, preferred_element_type=F32))
             output = jnp.dot(w3t_ref[...], hidden, preferred_element_type=F32)
@@ -185,27 +216,33 @@
             tangent = jnp.maximum(tangent, 0.0) + jnp.log(1.0 + jnp.exp(-jnp.abs(tangent)))
             output = jnp.concatenate([stress, tangent * (1.0 / PER_BLOCK)], axis=0).astype(BF16)
             for u in range(8):
-                prod_ref[part, 4 * half + u // 2, u % 2] = output[:, u * 128 : (u + 1) * 128]
-
-        @pl.when(part == 0)
-        def _():
-            pl.semaphore_wait(barrier, len(others))
-            lax.fori_loop(1, 16, send_index, 0)
-
-        for q in range(8):
-            dcore, dx, dy = ring_device(q)
-            slot = (1 - dcore) * (x * 2 + core) + dcore * (y * 2 + core)
-            if q == 7:
-                ring_ref[slot, part] = prod_ref[part, q]
+                prod_ref[part, 16 * h + 8 * half + u] = output[:, u * 128 : (u + 1) * 128]
+
+        if h == 0:
+
+            @pl.when(part == 0)
+            def _():
+                pl.semaphore_wait(barrier, 127)
+
+        for r, (along_z, at, slot) in enumerate(routes(h)):
+            first = 16 * h + (8 + r if along_z else 3 * r)
+            count = 1 if along_z else 3
+            source = prod_ref.at[part, pl.ds(first, count)]
+            target = ring_ref.at[slot, part, pl.ds(0 if along_z else 1, count)]
+            if h == 1 and r in (3, 7):
+                target[...] = source[...]
             else:
                 pltpu.make_async_remote_copy(
-                    src_ref=prod_ref.at[part, q],
-                    dst_ref=ring_ref.at[slot, part],
-                    send_sem=ring_send,
-                    recv_sem=ring_recv.at[slot, part],
-                    device_id=(dy * 2 + zh, (zl * 4 + dx) * 2 + dcore),
+                    src_ref=source,
+                    dst_ref=target,
+                    send_sem=ring_send.at[int(along_z)],
+                    recv_sem=ring_recv.at[int(along_z), slot, part],
+                    device_id=device(*at),
                     device_id_type=MESH,
                 ).start()
+
+        if h == 0:
+            pl.when(part == 0)(send_indices)
 
     mine = pick(x * 2 + core, y * 2 + core)
 
@@ -217,57 +254,55 @@
 
         for s in range(1, 8):
             slot = lax.rem(mine + s, 8)
-            got = ring_ref.at[slot, part]
-            pltpu.make_async_copy(got, got, ring_recv.at[slot, part]).wait()
-        for u in range(2):
-            t = lax.rem(place + part * 2 + u, 16)
-            owners = index_ref[t]
+            got = ring_ref.at[slot, part, pl.ds(1, 3)]
+            pltpu.make_async_copy(got, got, ring_recv.at[0, slot, part]).wait()
+            slot = lax.rem(z * 2 + core + s, 8)
+            got = ring_ref.at[slot, part, pl.ds(0, 1)]
+            pltpu.make_async_copy(got, got, ring_recv.at[1, slot, part]).wait()
+        for u in range(4):
+            owners = index_ref[part * 4 + u]
             block = lax.broadcasted_iota(jnp.int32, (256, 128), 0)
             onehot = jnp.concatenate(
                 [(block == owners[e : e + 1]).astype(F32).astype(BF16) for e in range(8)], axis=1
             )
             rows = jnp.concatenate([ring_ref[e, part, u] for e in range(8)], axis=1)
-            plane_out[t] = lax.dot_general(
+            plane_out[part * 4 + u] = lax.dot_general(
                 rows, onehot, (((1,), (1,)), ((), ())), preferred_element_type=F32
             ).astype(BF16)
-
-        def remote(u):
-            t = lax.rem(place + part * 2 + u, 16)
-            pltpu.make_async_remote_copy(
-                src_ref=plane_out.at[t],
-                dst_ref=plane_ref.at[place],
-                send_sem=plane_sem.at[0],
-                recv_sem=plane_sem.at[1],
-                device_id=plane_device(t),
-                device_id_type=MESH,
-            ).start()
-
-        pl.when(part > 0)(functools.partial(remote, 0))
-        remote(1)
-
-        @pl.when(part == 0)
+        for u in range(4):
+            here = y * 4 + x if u == 0 else pick(y, x) * 4 + z
+            self = jnp.logical_and(part == 0, kind == u)
+
+            @pl.when(self)
+            def _():
+                plane_ref[here] = plane_out[part * 4 + u]
+
+            @pl.when(jnp.logical_not(self))
+            def _():
+                pltpu.make_async_remote_copy(
+                    src_ref=plane_out.at[part * 4 + u],
+                    dst_ref=plane_ref.at[here],
+                    send_sem=plane_sem.at[0],
+                    recv_sem=plane_sem.at[1],
+                    device_id=device(*receiver(x, y, z, core, part, u), core),
+                    device_id_type=MESH,
+                ).start()
+
+    def run_part(part, carry):
+        network(part, 0)
+        network(part, 1)
+
+        @pl.when(part > 0)
         def _():
-            plane_ref[place] = plane_out[place]
-
-    def run_part(part, carry):
-        network(part)
-
-        @pl.when(part > 1)
-        def _():
-            reduce_rows(part - 2)
+            reduce_rows(part - 1)
 
         return carry
 
-    lax.fori_loop(0, 8, run_part, 0)
-
-    def run_rest(part, carry):
-        reduce_rows(part)
-        return carry
-
-    lax.fori_loop(6, 8, run_rest, 0)
+    lax.fori_loop(0, 4, run_part, 0)
+    reduce_rows(jnp.int32(3))
     for load in loads[1:]:
         load.wait()
-    jac_ref, off_ref, sum_ref, *krylov = (vectors.at[k] for k in range(8))
+    jac_ref, off_ref, sum_ref, back_ref, *krylov = (vectors.at[k] for k in range(9))
     for k in range(64):
         jac_ref[2 * k : 2 * k + 2, :] = e_ref[k, 2 * k : 2 * k + 2, :]
     pltpu.make_async_copy(plane_ref.at[pl.ds(0, 15)], plane_ref.at[pl.ds(0, 15)], plane_sem.at[1]).wait()
@@ -304,37 +339,37 @@
 
     def transposed_pass(tiles):
         def body(step, total):
-            for u in range(2):
-                k = step * 2 + u
+            for u in range(UNROLL):
+                k = step * UNROLL + u
                 total = total + tiles[k].reshape(16, 8, 128) * vb_ref[k][None]
             return total
 
-        return lax.fori_loop(0, 32, body, jnp.zeros((16, 8, 128), F32)).reshape(128, 128)
+        return lax.fori_loop(0, 64 // UNROLL, body, jnp.zeros((16, 8, 128), F32)).reshape(128, 128)
 
     def forward_pass(tiles, partner):
         partner = partner.reshape(16, 8, 128)
 
         def body(step, carry):
-            for u in range(2):
-                k = step * 2 + u
+            for u in range(UNROLL):
+                k = step * UNROLL + u
                 red_ref[k] += jnp.sum(tiles[k].reshape(16, 8, 128) * partner, axis=0)
             return carry
 
-        lax.fori_loop(0, 32, body, 0)
+        lax.fori_loop(0, 64 // UNROLL, body, 0)
 
     def both_pass(tiles, partner, first):
         partner = partner.reshape(16, 8, 128)
 
         def body(step, total):
-            for u in range(2):
-                k = step * 2 + u
+            for u in range(UNROLL):
+                k = step * UNROLL + u
                 tile = tiles[k].reshape(16, 8, 128)
                 forward = jnp.sum(tile * partner, axis=0)
                 red_ref[k] = forward if first else red_ref[k] + forward
                 total = total + tile * vb_ref[k][None]
             return total
 
-        return lax.fori_loop(0, 32, body, jnp.zeros((16, 8, 128), F32)).reshape(128, 128)
+        return lax.fori_loop(0, 64 // UNROLL, body, jnp.zeros((16, 8, 128), F32)).reshape(128, 128)
 
     index_b = i * 2 + zl
 
@@ -407,10 +442,15 @@
             ix, iy = out_x(it), out_y(it)
         acc_ref[...] += both_pass(e_ref, z, True)
         tmp_ref[EVEN, :], tmp_ref[ODD, :] = gather_p(z_even, z_odd, False)
-        tmp_ref[...] = both_pass(p_ref, tmp_ref[...], False)
-        add_even, add_odd = gather_p(tmp_ref[EVEN, :], tmp_ref[ODD, :], True)
-        acc_ref[EVEN, :] += add_even
-        acc_ref[ODD, :] += add_odd
+        back_ref[...] = both_pass(p_ref, tmp_ref[...], False)
+
+        def back_p():
+            add_even, add_odd = gather_p(back_ref[EVEN, :], back_ref[ODD, :], True)
+            acc_ref[EVEN, :] += add_even
+            acc_ref[ODD, :] += add_odd
+
+        if not last:
+            back_p()
         hx.wait_recv()
         tmp_ref[EVEN, :] = z_odd
         tmp_ref[ODD, :] = permute(hx_in[it], mx_ref[...], False) * edge_x
@@ -428,6 +468,7 @@
             sum_begin(moments + [z * (off_ref[...] * z + 2.0 * sum_ref[...])])
             ix, iy = out_x(it), out_y(it)
             sum_middle()
+            back_p()
         ix.wait_recv()
         acc_ref[EVEN, :] += ix_in[it] * start_x
         iy.wait_recv()
@@ -473,8 +514,10 @@
     for stage, (buffer, count) in enumerate([(sum_a, 7), (sum_b, 15)]):
         mover = buffer.at[pl.ds(0, count)]
         pltpu.make_async_copy(mover, mover, sum_send.at[stage]).wait()
-    out = prod_ref.at[pl.ds(0, 7)]
-    pltpu.make_async_copy(out, out, ring_send).wait()
+    out = prod_ref.at[pl.ds(0, 3), pl.ds(0, 28)]
+    pltpu.make_async_copy(out, out, ring_send.at[0]).wait()
+    out = prod_ref.at[0, pl.ds(0, 28)]
+    pltpu.make_async_copy(out, out, ring_send.at[1]).wait()
     pltpu.make_async_copy(plane_ref.at[pl.ds(0, 15)], plane_ref.at[pl.ds(0, 15)], plane_sem.at[0]).wait()
     pltpu.make_async_copy(index_ref.at[pl.ds(0, 15)], index_ref.at[pl.ds(0, 15)], index_sem.at[0]).wait()
 
@@ -522,8 +565,8 @@
             pltpu.VMEM((512, 64), BF16),
             pltpu.VMEM((512, 512), BF16),
             pltpu.VMEM((128, 512), BF16),
-            pltpu.VMEM((8, 8, 2, 128, 128), BF16),
-            pltpu.VMEM((8, 8, 2, 128, 128), BF16),
+            pltpu.VMEM((4, 32, 128, 128), BF16),
+            pltpu.VMEM((8, 4, 4, 128, 128), BF16),
             pltpu.VMEM((16, 128, 256), BF16),
             pltpu.VMEM((16, 128, 256), BF16),
             pltpu.VMEM((16, 8, 128), jnp.int32),
@@ -534,7 +577,7 @@
             tile,
             pltpu.VMEM((256, 256), BF16),
             pltpu.VMEM((128, 128), BF16),
-            pltpu.VMEM((8, 128, 128), F32),
+            pltpu.VMEM((9, 128, 128), F32),
             pltpu.VMEM((64, 8, 128), F32),
             pltpu.VMEM((64, 8, 128), F32),
             square,
@@ -550,8 +593,8 @@
             pltpu.VMEM((8, 8, 128), F32),
             pltpu.VMEM((16, 8, 128), F32),
             dma((5,)),
-            dma,
-            dma((8, 8)),
+            dma((2,)),
+            dma((2, 8, 4)),
             dma((2,)),
             dma((2,)),
             dma((4 * ITERS,)),

time: 76.4 us -> 81.6 us (1.068)
  Pallas kernels: 75.6 us -> 80.8 us
    pallas_call x1, Pallas kernels: 74.1 us -> 79.2 us  [local(): pl.pallas_call(kernel, out_shape=[jax.ShapeDtypeStruct((128, 128), F32)]...]
where the time goes in v5:
time: 81.6 us; the launch traced here: 81.4 us
  Pallas kernels  80.8 us (99%)
    pallas_call x1, Pallas kernels, local(): pl.pallas_call(kernel, out_shape=[jax.ShapeDtypeStruct((128, 128), F32)]...  79.2 us

profile of v5, /device:TPU:1, one launch (start us, length us, event | category | flops | bytes accessed | tf_op | source)
XLA Modules:
  0.0 81.4 jit_solution(15954925923958964415)
XLA Ops:
  0.6 79.2 %shard_map.131 = (f32[128,128]{1,0:T(8,128)}, f32[128,128]{1,0:T(8,128)}) custom-call(bf16[64,16384]{1,0:T(8,128)(2,1)} %bitcast.17, bf16[64,512]{1,0:T(8,128)(2,1)} %w1_ref.1, bf16[512,512]{1,0:T(8,128)(2,1)} %w2_ref.1, bf16[512,128]{1,0:T(8,128)(2,1)} %w3_ref.1, s32[128,128]{1,0:T(8,128)} %bitcast.18, f32[64,128,128]{2,1,0:T(8,128)} %bitcast.13, ...), custom_call_target="tpu_custom_call" | custom-call | tf_op jit(solution)/shard_map/pallas_call | solution.py:558
  79.9 1.5 %shard_map.132 = (f32[128,128]{1,0:T(8,128)}, f32[128,128]{1,0:T(8,128)}) custom-call(f32[128,128]{1,0:T(8,128)} %get-tuple-element.6.adjoint_ref, f32[128,128]{1,0:T(8,128)} %get-tuple-element.7.residual_ref), custom_call_target="tpu_custom_call" | custom-call | tf_op jit(solution)/shard_map/pallas_call | solution.py:609

commit v6 on v4

--- a/solution.py
+++ b/solution.py
@@ -9,6 +9,7 @@
 
 FEATURES = 64
 ITERS = 3
+UNROLL = 8
 PER_BLOCK = 64
 DIAG_SHIFT = 5.0
 MESH = pl.DeviceIdType.MESH
@@ -190,7 +191,6 @@
         @pl.when(part == 0)
         def _():
             pl.semaphore_wait(barrier, len(others))
-            lax.fori_loop(1, 16, send_index, 0)
 
         for q in range(8):
             dcore, dx, dy = ring_device(q)
@@ -206,6 +206,10 @@
                     device_id=(dy * 2 + zh, (zl * 4 + dx) * 2 + dcore),
                     device_id_type=MESH,
                 ).start()
+
+        @pl.when(part == 0)
+        def _():
+            lax.fori_loop(1, 16, send_index, 0)
 
     mine = pick(x * 2 + core, y * 2 + core)
 
@@ -267,7 +271,7 @@
     lax.fori_loop(6, 8, run_rest, 0)
     for load in loads[1:]:
         load.wait()
-    jac_ref, off_ref, sum_ref, *krylov = (vectors.at[k] for k in range(8))
+    jac_ref, off_ref, sum_ref, back_ref, *krylov = (vectors.at[k] for k in range(9))
     for k in range(64):
         jac_ref[2 * k : 2 * k + 2, :] = e_ref[k, 2 * k : 2 * k + 2, :]
     pltpu.make_async_copy(plane_ref.at[pl.ds(0, 15)], plane_ref.at[pl.ds(0, 15)], plane_sem.at[1]).wait()
@@ -304,37 +308,37 @@
 
     def transposed_pass(tiles):
         def body(step, total):
-            for u in range(2):
-                k = step * 2 + u
+            for u in range(UNROLL):
+                k = step * UNROLL + u
                 total = total + tiles[k].reshape(16, 8, 128) * vb_ref[k][None]
             return total
 
-        return lax.fori_loop(0, 32, body, jnp.zeros((16, 8, 128), F32)).reshape(128, 128)
+        return lax.fori_loop(0, 64 // UNROLL, body, jnp.zeros((16, 8, 128), F32)).reshape(128, 128)
 
     def forward_pass(tiles, partner):
         partner = partner.reshape(16, 8, 128)
 
         def body(step, carry):
-            for u in range(2):
-                k = step * 2 + u
+            for u in range(UNROLL):
+                k = step * UNROLL + u
                 red_ref[k] += jnp.sum(tiles[k].reshape(16, 8, 128) * partner, axis=0)
             return carry
 
-        lax.fori_loop(0, 32, body, 0)
+        lax.fori_loop(0, 64 // UNROLL, body, 0)
 
     def both_pass(tiles, partner, first):
         partner = partner.reshape(16, 8, 128)
 
         def body(step, total):
-            for u in range(2):
-                k = step * 2 + u
+            for u in range(UNROLL):
+                k = step * UNROLL + u
                 tile = tiles[k].reshape(16, 8, 128)
                 forward = jnp.sum(tile * partner, axis=0)
                 red_ref[k] = forward if first else red_ref[k] + forward
                 total = total + tile * vb_ref[k][None]
             return total
 
-        return lax.fori_loop(0, 32, body, jnp.zeros((16, 8, 128), F32)).reshape(128, 128)
+        return lax.fori_loop(0, 64 // UNROLL, body, jnp.zeros((16, 8, 128), F32)).reshape(128, 128)
 
     index_b = i * 2 + zl
 
@@ -407,10 +411,15 @@
             ix, iy = out_x(it), out_y(it)
         acc_ref[...] += both_pass(e_ref, z, True)
         tmp_ref[EVEN, :], tmp_ref[ODD, :] = gather_p(z_even, z_odd, False)
-        tmp_ref[...] = both_pass(p_ref, tmp_ref[...], False)
-        add_even, add_odd = gather_p(tmp_ref[EVEN, :], tmp_ref[ODD, :], True)
-        acc_ref[EVEN, :] += add_even
-        acc_ref[ODD, :] += add_odd
+        back_ref[...] = both_pass(p_ref, tmp_ref[...], False)
+
+        def back_p():
+            add_even, add_odd = gather_p(back_ref[EVEN, :], back_ref[ODD, :], True)
+            acc_ref[EVEN, :] += add_even
+            acc_ref[ODD, :] += add_odd
+
+        if not last:
+            back_p()
         hx.wait_recv()
         tmp_ref[EVEN, :] = z_odd
         tmp_ref[ODD, :] = permute(hx_in[it], mx_ref[...], False) * edge_x
@@ -428,6 +437,7 @@
             sum_begin(moments + [z * (off_ref[...] * z + 2.0 * sum_ref[...])])
             ix, iy = out_x(it), out_y(it)
             sum_middle()
+            back_p()
         ix.wait_recv()
         acc_ref[EVEN, :] += ix_in[it] * start_x
         iy.wait_recv()
@@ -534,7 +544,7 @@
             tile,
             pltpu.VMEM((256, 256), BF16),
             pltpu.VMEM((128, 128), BF16),
-            pltpu.VMEM((8, 128, 128), F32),
+            pltpu.VMEM((9, 128, 128), F32),
             pltpu.VMEM((64, 8, 128), F32),
             pltpu.VMEM((64, 8, 128), F32),
             square,

time: 76.4 us -> 74.3 us (0.973)
  Pallas kernels: 75.6 us -> 73.4 us
    pallas_call x1, Pallas kernels: 74.1 us -> 71.9 us  [local(): pl.pallas_call(kernel, out_shape=[jax.ShapeDtypeStruct((128, 128), F32)]...]
where the time goes in v6:
time: 74.3 us; the launch traced here: 74.1 us
  Pallas kernels  73.4 us (99%)
    pallas_call x1, Pallas kernels, local(): pl.pallas_call(kernel, out_shape=[jax.ShapeDtypeStruct((128, 128), F32)]...  71.9 us
    pallas_call x1, Pallas kernels, local(): pl.pallas_call(hand_over, out_shape=[jax.ShapeDtypeStruct((128, 128), F32...  1.53 us

profile of v6, /device:TPU:1, one launch (start us, length us, event | category | flops | bytes accessed | tf_op | source)
XLA Modules:
  0.0 74.1 jit_solution(4342095818301980462)
XLA Ops:
  0.6 71.9 %shard_map.131 = (f32[128,128]{1,0:T(8,128)}, f32[128,128]{1,0:T(8,128)}) custom-call(bf16[64,16384]{1,0:T(8,128)(2,1)} %bitcast.17, bf16[64,512]{1,0:T(8,128)(2,1)} %w1_ref.1, bf16[512,512]{1,0:T(8,128)(2,1)} %w2_ref.1, bf16[512,128]{1,0:T(8,128)(2,1)} %w3_ref.1, s32[128,128]{1,0:T(8,128)} %bitcast.18, f32[64,128,128]{2,1,0:T(8,128)} %bitcast.13, ...), custom_call_target="tpu_custom_call" | custom-call | tf_op jit(solution)/shard_map/pallas_call | solution.py:525
  72.5 1.5 %shard_map.132 = (f32[128,128]{1,0:T(8,128)}, f32[128,128]{1,0:T(8,128)}) custom-call(f32[128,128]{1,0:T(8,128)} %get-tuple-element.6.adjoint_ref, f32[128,128]{1,0:T(8,128)} %get-tuple-element.7.residual_ref), custom_call_target="tpu_custom_call" | custom-call | tf_op jit(solution)/shard_map/pallas_call | solution.py:576

commit v7 on v6

--- a/solution.py
+++ b/solution.py
@@ -315,13 +315,14 @@
 
         return lax.fori_loop(0, 64 // UNROLL, body, jnp.zeros((16, 8, 128), F32)).reshape(128, 128)
 
-    def forward_pass(tiles, partner):
+    def forward_pass(tiles, partner, first=False):
         partner = partner.reshape(16, 8, 128)
 
         def body(step, carry):
             for u in range(UNROLL):
                 k = step * UNROLL + u
-                red_ref[k] += jnp.sum(tiles[k].reshape(16, 8, 128) * partner, axis=0)
+                forward = jnp.sum(tiles[k].reshape(16, 8, 128) * partner, axis=0)
+                red_ref[k] = forward if first else red_ref[k] + forward
             return carry
 
         lax.fori_loop(0, 64 // UNROLL, body, 0)
@@ -401,17 +402,24 @@
         z_even, z_odd = tmp_ref[EVEN, :], tmp_ref[ODD, :]
         hx_out[it] = z_even
         hx = send(hx_out.at[it], hx_in.at[it], 4 * it, x_prev)
-        hy_out[it] = z.T[0:8]
-        hy = send(hy_out.at[it], hy_in.at[it], 4 * it + 1, y_prev)
         for q in range(4):
             vb_ref[:, 2 * q, :] = z_even
             vb_ref[:, 2 * q + 1, :] = z_odd
         acc_ref[...] = off_ref[...] * z
         if not last:
-            ix, iy = out_x(it), out_y(it)
-        acc_ref[...] += both_pass(e_ref, z, True)
+            ix = out_x(it)
+        hy_out[it] = z.T[0:8]
+        hy = send(hy_out.at[it], hy_in.at[it], 4 * it + 1, y_prev)
+        if last:
+            forward_pass(e_ref, z, True)
+        else:
+            iy = out_y(it)
+            acc_ref[...] += both_pass(e_ref, z, True)
         tmp_ref[EVEN, :], tmp_ref[ODD, :] = gather_p(z_even, z_odd, False)
-        back_ref[...] = both_pass(p_ref, tmp_ref[...], False)
+        if last:
+            forward_pass(p_ref, tmp_ref[...])
+        else:
+            back_ref[...] = both_pass(p_ref, tmp_ref[...], False)
 
         def back_p():
             add_even, add_odd = gather_p(back_ref[EVEN, :], back_ref[ODD, :], True)
@@ -437,6 +445,8 @@
             sum_begin(moments + [z * (off_ref[...] * z + 2.0 * sum_ref[...])])
             ix, iy = out_x(it), out_y(it)
             sum_middle()
+            acc_ref[...] += transposed_pass(e_ref)
+            back_ref[...] = transposed_pass(p_ref)
             back_p()
         ix.wait_recv()
         acc_ref[EVEN, :] += ix_in[it] * start_x
@@ -489,9 +499,15 @@
     pltpu.make_async_copy(index_ref.at[pl.ds(0, 15)], index_ref.at[pl.ds(0, 15)], index_sem.at[0]).wait()
 
 
-def hand_over(adjoint_ref, residual_ref, adjoint_out, residual_out):
-    adjoint_out[...] = adjoint_ref[...]
-    residual_out[...] = residual_ref[...]
+def hand_over(adjoint_ref, residual_ref, adjoint_out, residual_out, sems):
+    copies = [
+        pltpu.make_async_copy(adjoint_ref, adjoint_out, sems.at[0]),
+        pltpu.make_async_copy(residual_ref, residual_out, sems.at[1]),
+    ]
+    for copy in copies:
+        copy.start()
+    for copy in copies:
+        copy.wait()
 
 
 def local(*args):
@@ -576,8 +592,9 @@
     adjoint, residual = pl.pallas_call(
         hand_over,
         out_shape=[jax.ShapeDtypeStruct((128, 128), F32)] * 2,
-        in_specs=[vmem, vmem],
-        out_specs=[vmem, vmem],
+        in_specs=[hbm, hbm],
+        out_specs=[hbm, hbm],
+        scratch_shapes=[dma((2,))],
     )(adjoint, residual)
     return adjoint.reshape(64, 2, 128), residual.reshape(64, 2, 128)
 

time: 74.3 us -> 77.8 us (1.047)
  Pallas kernels: 73.4 us -> 77 us
    pallas_call x1, Pallas kernels: 1.53 us -> 5.09 us  [local(): pl.pallas_call(hand_over, out_shape=[jax.ShapeDtypeStruct((128, 128), F32...]
where the time goes in v7:
time: 77.8 us; the launch traced here: 77.6 us
  Pallas kernels  77 us (99%)
    pallas_call x1, Pallas kernels, local(): pl.pallas_call(kernel, out_shape=[jax.ShapeDtypeStruct((128, 128), F32)]...  71.9 us
    pallas_call x1, Pallas kernels, local(): pl.pallas_call(hand_over, out_shape=[jax.ShapeDtypeStruct((128, 128), F32...  5.09 us

profile of v7, /device:TPU:1, one launch (start us, length us, event | category | flops | bytes accessed | tf_op | source)
XLA Modules:
  0.0 77.6 jit_solution(16780284211310375634)
XLA Ops:
  0.6 71.9 %shard_map.131 = (f32[128,128]{1,0:T(8,128)}, f32[128,128]{1,0:T(8,128)}) custom-call(bf16[64,16384]{1,0:T(8,128)(2,1)} %bitcast.17, bf16[64,512]{1,0:T(8,128)(2,1)} %w1_ref.1, bf16[512,512]{1,0:T(8,128)(2,1)} %w2_ref.1, bf16[512,128]{1,0:T(8,128)(2,1)} %w3_ref.1, s32[128,128]{1,0:T(8,128)} %bitcast.18, f32[64,128,128]{2,1,0:T(8,128)} %bitcast.13, ...), custom_call_target="tpu_custom_call" | custom-call | tf_op jit(solution)/shard_map/pallas_call | solution.py:541
  72.5 5.1 %shard_map.132 = (f32[128,128]{1,0:T(8,128)}, f32[128,128]{1,0:T(8,128)}) custom-call(f32[128,128]{1,0:T(8,128)} %get-tuple-element.6.adjoint_ref, f32[128,128]{1,0:T(8,128)} %get-tuple-element.7.residual_ref), custom_call_target="tpu_custom_call" | custom-call | tf_op jit(solution)/shard_map/pallas_call | solution.py:592

commit v8 on v7

--- a/solution.py
+++ b/solution.py
@@ -9,7 +9,7 @@
 
 FEATURES = 64
 ITERS = 3
-UNROLL = 8
+UNROLL = 16
 PER_BLOCK = 64
 DIAG_SHIFT = 5.0
 MESH = pl.DeviceIdType.MESH
@@ -499,15 +499,9 @@
     pltpu.make_async_copy(index_ref.at[pl.ds(0, 15)], index_ref.at[pl.ds(0, 15)], index_sem.at[0]).wait()
 
 
-def hand_over(adjoint_ref, residual_ref, adjoint_out, residual_out, sems):
-    copies = [
-        pltpu.make_async_copy(adjoint_ref, adjoint_out, sems.at[0]),
-        pltpu.make_async_copy(residual_ref, residual_out, sems.at[1]),
-    ]
-    for copy in copies:
-        copy.start()
-    for copy in copies:
-        copy.wait()
+def hand_over(adjoint_ref, residual_ref, adjoint_out, residual_out):
+    adjoint_out[...] = adjoint_ref[...]
+    residual_out[...] = residual_ref[...]
 
 
 def local(*args):
@@ -592,9 +586,8 @@
     adjoint, residual = pl.pallas_call(
         hand_over,
         out_shape=[jax.ShapeDtypeStruct((128, 128), F32)] * 2,
-        in_specs=[hbm, hbm],
-        out_specs=[hbm, hbm],
-        scratch_shapes=[dma((2,))],
+        in_specs=[vmem, vmem],
+        out_specs=[vmem, vmem],
     )(adjoint, residual)
     return adjoint.reshape(64, 2, 128), residual.reshape(64, 2, 128)
 

time: 77.8 us -> 74 us (0.951)
  Pallas kernels: 77 us -> 73.2 us
    pallas_call x1, Pallas kernels: 5.09 us -> 1.53 us  [local(): pl.pallas_call(hand_over, out_shape=[jax.ShapeDtypeStruct((128, 128), F32...]
where the time goes in v8:
time: 74 us; the launch traced here: 73.9 us
  Pallas kernels  73.2 us (99%)
    pallas_call x1, Pallas kernels, local(): pl.pallas_call(kernel, out_shape=[jax.ShapeDtypeStruct((128, 128), F32)]...  71.7 us
    pallas_call x1, Pallas kernels, local(): pl.pallas_call(hand_over, out_shape=[jax.ShapeDtypeStruct((128, 128), F32...  1.53 us

profile of v8, /device:TPU:1, one launch (start us, length us, event | category | flops | bytes accessed | tf_op | source)
XLA Modules:
  0.0 73.9 jit_solution(11076867127017266276)
XLA Ops:
  0.6 71.7 %shard_map.131 = (f32[128,128]{1,0:T(8,128)}, f32[128,128]{1,0:T(8,128)}) custom-call(bf16[64,16384]{1,0:T(8,128)(2,1)} %bitcast.17, bf16[64,512]{1,0:T(8,128)(2,1)} %w1_ref.1, bf16[512,512]{1,0:T(8,128)(2,1)} %w2_ref.1, bf16[512,128]{1,0:T(8,128)(2,1)} %w3_ref.1, s32[128,128]{1,0:T(8,128)} %bitcast.18, f32[64,128,128]{2,1,0:T(8,128)} %bitcast.13, ...), custom_call_target="tpu_custom_call" | custom-call | tf_op jit(solution)/shard_map/pallas_call | solution.py:535
  72.3 1.5 %shard_map.132 = (f32[128,128]{1,0:T(8,128)}, f32[128,128]{1,0:T(8,128)}) custom-call(f32[128,128]{1,0:T(8,128)} %get-tuple-element.6.adjoint_ref, f32[128,128]{1,0:T(8,128)} %get-tuple-element.7.residual_ref), custom_call_target="tpu_custom_call" | custom-call | tf_op jit(solution)/shard_map/pallas_call | solution.py:586
